TPU v7x, 512 devices: a whole 4x4x16 slice. The times are simulated.
512 devices in a mesh: cube: 64 (over z, x_lo, core), sub: 8 (over y, x_hi).
Axes of the slice: x: 4 (x_hi: 2, x_lo: 2; x = x_hi * 2 + x_lo), y: 4, z: 16, core: 2. Of those that a mesh axis runs over, the one named last changes fastest.
Arguments:
- leaf_fronts: bfloat16 [16384, 2048], P('cube', 'sub'), may hold values from -8 to 8, as said below
- pivot_entries: bfloat16 [7, 256, 256], replicated, may hold values from -8 to 8, as said below
- pivot_inverse: bfloat16 [15, 2, 128, 128], replicated, as said below
- block_map_one: int32 [4, 2, 14], replicated, may hold values from 0 to 31, as said below
- block_map_two: int32 [2, 2, 30], replicated, may hold values from 0 to 63, as said below
- block_map_top: int32 [1, 2, 62], replicated, may hold values from 0 to 127, as said below
Outputs:
- top_front: bfloat16 [16384, 16384], P('cube', 'sub')
Inputs may be any that keep to these rules, and one draw needn't show every extreme that they name: `leaf_fronts`: each front is symmetric in natural order. `pivot_entries`: each pivot block pair is symmetric. `pivot_inverse`: each inverse is symmetric. `block_map_one`: for each front and child the entries are distinct, and entry i is congruent to i + 2 modulo 8; parent block 1 receives a block of the second child. `block_map_two`: for each front and child the entries are distinct, and entry i is congruent to i + 2 modulo 2 * 8; parent block 1 receives a block of the second child. `block_map_top`: for each child the entries are distinct, and entry i is congruent to i + 2 modulo 4 * 8; parent block 1 receives a block of the second child.
All inputs are finite; a program needn't handle non-finite values.
Results may differ from a plain program's by a relative error of at most 0.025.
Values may be sent and summed in bfloat16 or wider, within the bound.
No kernel may reach another device: no remote copies, remote signals or barrier semaphores. Data moves between devices by JAX's collectives and lax.ppermute only.
A program may use at most 64 MiB of HBM per device.

v0:
```python
import jax
import jax.numpy as jnp
from jax import lax
from jax.experimental import pallas as pl
from jax.experimental.pallas import tpu as pltpu
from jax.sharding import Mesh, PartitionSpec as P

BLOCK = 128
CHUNK = 256
F32 = jnp.float32
BF16 = jnp.bfloat16
MAP_START = (3, 3 + 112, 3 + 112 + 120)


def dot(lhs, rhs):
    return jnp.dot(lhs, rhs, preferred_element_type=F32)


def dot_tn(lhs, rhs):
    return lax.dot_general(lhs, rhs, (((0,), (0,)), ((), ())), preferred_element_type=F32)


def panels(first, second, inverse_zero, inverse_one, row_one):
    scaled_zero = dot(inverse_zero, first).astype(BF16)
    coupling = first[:, row_one : row_one + BLOCK]
    col_one = (second.astype(F32) - dot_tn(coupling, scaled_zero)).astype(BF16)
    scaled_one = dot(inverse_one, col_one).astype(BF16)
    columns = jnp.concatenate([first, col_one], 0)
    scaled = jnp.concatenate([scaled_zero, scaled_one], 0)
    return columns, scaled


def upper_kernel(
    info, whole, got, mine, other, pivots, inverses, out,
    z_one, z_two, z_top, y_one, y_two, y_top, t_one, t_two, own_one, own_two, core_one, core_two,
):
    p, s, c = info[0], info[1], info[2]
    z_refs = (None, z_one, z_two, z_top)
    y_refs = (None, y_one, y_two, y_top)
    t_refs = (None, t_one, t_two)
    own_refs = (None, own_one, own_two)
    core_refs = (None, core_one, core_two)

    def entry(level, front, child, index):
        count = (8 << level) - 2
        return info[MAP_START[level - 1] + (front * 2 + child) * count + index]

    def find(level, front, child, wanted):
        group = 4 << level
        low = lax.rem(p, group)
        first = entry(level, front, child, jnp.maximum(low - 2, 0))
        second = entry(level, front, child, low + group - 2)
        spot = jnp.where(second == wanted, low + group, -1)
        return jnp.where((low >= 2) & (first == wanted), low, spot)

    slots = {(3, 0): [p, p + 64]}
    for level in (3, 2, 1):
        for front in range(16 >> level):
            slots[level - 1, front] = [
                find(level, front // 2, front % 2, spot) for spot in slots[level, front // 2]
            ]

    def leaf_slots(front, wide):
        parts = []
        for spot in slots[0, front]:
            part = jnp.where(spot >= 8, wide[:, BLOCK:], wide[:, :BLOCK])
            parts.append(jnp.where(spot >= 0, part, jnp.zeros_like(part)))
        return jnp.concatenate(parts, 1)

    def leaf_own(front, q):
        stacked = [got[sub, front, 16 * q : 16 * q + 16, :] for sub in range(8)]
        return leaf_slots(front, jnp.concatenate(stacked, 0))

    def leaf_core(front):
        return jnp.concatenate([got[sub, front, 32:64, :] for sub in range(8)], 0)

    for level in (1, 2, 3):
        z_ref, y_ref = z_refs[level], y_refs[level]
        group = 4 << level
        width = 256 << level
        wanted = 4 if level < 3 else 2
        z_ref[...] = jnp.zeros_like(z_ref)
        y_ref[...] = jnp.zeros_like(y_ref)
        for front in range(8 >> level):
            kids = (2 * front, 2 * front + 1)
            goal = (0, 1, 2 * group, 2 * group + 1)
            mask = [
                [entry(level, front, child, group - 2 + q % 2) == goal[q] for q in range(4)]
                for child in range(2)
            ]

            def masked(child, q, value):
                return jnp.where(mask[child][q], value, jnp.zeros_like(value))

            for child, kid in enumerate(kids):
                def put(block, dest, panel, row):
                    spread = [
                        masked(child, q, panel[:, (q % 2) * BLOCK : (q % 2 + 1) * BLOCK])
                        for q in range(wanted)
                    ]
                    spread = jnp.concatenate(spread, 1)
                    at = pl.ds(pl.multiple_of(dest * 16, 16), 16)
                    if child == 1:
                        spread = spread + z_ref[front, at, :]
                        row = row + y_ref[front, at, :]
                    z_ref[front, at, :] = spread
                    y_ref[front, at, :] = row

                if level == 1:
                    for block in range(2, 16):
                        here = (block // 4, kid, pl.ds(16 * (block % 2), 16))
                        panel = jnp.where(c == block // 2 % 2, mine[here], other[here])
                        row = leaf_slots(kid, whole[kid, 16 * block : 16 * block + 16, :])
                        put(block, entry(level, front, child, block - 2), panel, row)
                else:
                    def step(block, carry):
                        at = pl.ds(pl.multiple_of(block * 16, 16), 16)
                        put(
                            block,
                            entry(level, front, child, block - 2),
                            t_refs[level - 1][kid, at, :],
                            y_refs[level - 1][kid, at, :],
                        )
                        return carry

                    lax.fori_loop(2, 2 * group, step, 0, unroll=6)

            if level == 3:
                lane_part = []
                for half in range(2):
                    at = pl.ds(pl.multiple_of(half * BLOCK + 16 * s, 16), 16)
                    strip = pivots[6, at, :]
                    z_ref[0, 16 * half : 16 * half + 16, :] += strip
                    strip = jnp.where(p == 0, strip[:, :BLOCK], strip[:, BLOCK:])
                    strip = jnp.where(p < 2, strip, jnp.zeros_like(strip))
                    y_ref[0, 16 * half : 16 * half + 16, :BLOCK] += strip

            core_rows = (2, 3, 1) if level < 3 else (1,)
            zt = []
            for q in range(wanted):
                parts = []
                own = jnp.zeros((BLOCK, 256), F32)
                for child, kid in enumerate(kids):
                    if level == 1:
                        value = leaf_own(kid, q % 2)
                    else:
                        value = own_refs[level - 1][kid, (q % 2) * BLOCK : (q % 2 + 1) * BLOCK, :]
                    own = own + masked(child, q, value.astype(F32))
                if level == 3:
                    strip = pivots[6, q * BLOCK : (q + 1) * BLOCK, :].astype(F32)
                    strip = jnp.where(p == 0, strip[:, :BLOCK], strip[:, BLOCK:])
                    strip = jnp.where(p < 2, strip, jnp.zeros_like(strip))
                    own = own + jnp.concatenate([strip, jnp.zeros_like(strip)], 1)
                parts.append(own)
                for r in core_rows:
                    value = jnp.zeros((BLOCK, BLOCK), F32)
                    for child, kid in enumerate(kids):
                        if level == 1:
                            part = leaf_core(kid)[(q % 2) * BLOCK : (q % 2 + 1) * BLOCK]
                        else:
                            part = core_refs[level - 1][kid, (q % 2) * BLOCK : (q % 2 + 1) * BLOCK, :]
                        part = part[:, (r % 2) * BLOCK : (r % 2 + 1) * BLOCK].astype(F32)
                        value = value + masked(child, q, masked(child, r, part))
                    if q == 0 and r == 1:
                        value = value + pivots[
                            8 - (16 >> level) + front, :BLOCK, BLOCK:
                        ].astype(F32)
                    parts.append(value)
                zt.append(jnp.concatenate(parts, 1).astype(BF16))
            live = zt[0].shape[1] - BLOCK
            inverse_zero = inverses[16 - (16 >> level) + front, 0]
            inverse_one = inverses[16 - (16 >> level) + front, 1]
            columns, scaled = panels(zt[0], zt[1], inverse_zero, inverse_one, live)
            coupling = columns[:BLOCK, live:]
            own_scaled = scaled[:, :256]
            if level < 3:
                core_cols = columns[:, 256:512]
                later = jnp.concatenate([zt[2], zt[3]], 0)[:, :512].astype(F32)
                later = (later - dot_tn(core_cols, scaled[:, :512])).astype(BF16)
                own_refs[level][front] = later[:, :256]
                core_refs[level][front] = later[:, 256:]
            for start in range(0, width, CHUNK):
                at = pl.ds(start, CHUNK)
                first = z_ref[front, at, :BLOCK]
                scaled_zero = dot(first, inverse_zero).astype(BF16)
                second = z_ref[front, at, BLOCK : 2 * BLOCK].astype(F32)
                second = (second - dot(scaled_zero, coupling)).astype(BF16)
                row = y_ref[front, at, :].astype(F32)
                row = row - dot(jnp.concatenate([first, second], 1), own_scaled)
                if level == 3:
                    out[:, start : start + CHUNK] = row.T.astype(BF16)
                    continue
                y_ref[front, at, :] = row.astype(BF16)
                scaled_one = dot(second, inverse_one).astype(BF16)
                rest = z_ref[front, at, 2 * BLOCK :].astype(F32)
                rest = rest - dot(jnp.concatenate([scaled_zero, scaled_one], 1), core_cols)
                t_refs[level][front, at, :] = rest.astype(BF16)


def upper_levels(info, whole, got, mine, other, pivots, inverses):
    vmem = pl.BlockSpec(memory_space=pltpu.VMEM)
    return pl.pallas_call(
        upper_kernel,
        out_shape=jax.ShapeDtypeStruct((256, 2048), BF16),
        in_specs=[pl.BlockSpec(memory_space=pltpu.SMEM)] + [vmem] * 6,
        out_specs=vmem,
        scratch_shapes=[
            pltpu.VMEM(shape, BF16)
            for shape in (
                (4, 512, 512), (2, 1024, 512), (1, 2048, 256),
                (4, 512, 256), (2, 1024, 256), (1, 2048, 256),
                (4, 512, 256), (2, 1024, 256),
                (4, 256, 256), (2, 256, 256), (4, 256, 256), (2, 256, 256),
            )
        ],
        compiler_params=pltpu.CompilerParams(vmem_limit_bytes=48 * 2**20),
        name="upper_levels",
    )(info, whole, got, mine, other, pivots, inverses)


def gather_ring(payload, k, count):
    parts = [(payload, k)]
    ahead = behind = payload
    up = [(i, (i + 1) % count) for i in range(count)]
    down = [(i, (i - 1) % count) for i in range(count)]
    for step in range(1, count // 2 + 1):
        ahead = lax.ppermute(ahead, "k", up)
        parts.append((ahead, (k - step) % count))
        if step < count // 2:
            behind = lax.ppermute(behind, "k", down)
            parts.append((behind, (k + step) % count))
    whole = jnp.zeros((count,) + payload.shape, payload.dtype)
    for part, spot in parts:
        whole = lax.dynamic_update_slice_in_dim(whole, part[None], spot, 0)
    return whole


def leaf_stage(leaf, inverses, zl, xl, c, u, s):
    tile = leaf
    spread = jnp.where(xl == 0, tile, lax.ppermute(tile, "xl", [(0, 1)]))
    spread = jnp.where(zl == 0, spread, lax.ppermute(spread, "zl", [(0, 1)]))
    other = lax.ppermute(spread, "c", [(0, 1), (1, 0)])
    even = jnp.where(c == 0, spread, other)
    odd = jnp.where(c == 0, other, spread)
    piece = jnp.concatenate(
        [
            tile[:, :32],
            odd[:BLOCK, :32],
            even[BLOCK:, :32],
            odd[BLOCK:, :32],
            even[BLOCK:, 128:160],
            odd[BLOCK:, 128:160],
        ],
        0,
    ).T
    got = lax.all_to_all(jnp.broadcast_to(piece[None], (8,) + piece.shape), "sub", 0, 0, tiled=True)
    got = got.reshape(8, 2, 16, 896).transpose(1, 0, 2, 3).reshape(2, BLOCK, 896)
    first = jnp.concatenate([even[:BLOCK], got[0, :, :640]], 1)
    second = jnp.concatenate([odd[:BLOCK], got[1, :, :640]], 1)
    columns, scaled = panels(first, second, inverses[0], inverses[1], 512)
    core = got[:, :, 640:].reshape(256, 256).astype(F32)
    core = core - dot_tn(columns[:, 640:], scaled[:, 640:])
    cols = jnp.concatenate([even[BLOCK:], odd[BLOCK:]], 0).T.astype(F32)
    cols = cols - dot_tn(scaled[:, :256], columns[:, 640:])
    tile = tile.T.astype(F32) - dot_tn(columns[:, :256], scaled[:, 256:512])
    return jnp.concatenate(
        [
            tile.astype(BF16),
            lax.dynamic_slice_in_dim(core.astype(BF16), 32 * s, 32, 0),
            lax.dynamic_slice_in_dim(cols.astype(BF16), 32 * u, 32, 0),
        ],
        0,
    )


def local(leaf_fronts, pivot_entries, pivot_inverse, block_map_one, block_map_two, block_map_top):
    k, zl, xl, c = (lax.axis_index(name) for name in ("k", "zl", "xl", "c"))
    s = lax.axis_index("sub")
    u = zl * 4 + xl * 2 + c
    maps = (block_map_one, block_map_two, block_map_top)
    info = jnp.concatenate(
        [jnp.stack([k * 8 + u, s, c]).astype(jnp.int32)] + [table.reshape(-1) for table in maps]
    )
    payload = leaf_stage(
        leaf_fronts, lax.dynamic_index_in_dim(pivot_inverse, k, 0, keepdims=False), zl, xl, c, u, s
    )
    whole = gather_ring(payload, k, 8)
    mine = lax.all_to_all(
        jnp.broadcast_to(whole[None, :, 288:], (4, 8, 32, 256)), ("zl", "xl"), 0, 0, tiled=True
    )
    other = lax.ppermute(mine, "c", [(0, 1), (1, 0)])
    piece = jnp.concatenate([whole[:, 128:160], whole[:, 256:288]], 1)
    got = lax.all_to_all(jnp.broadcast_to(piece[None], (8, 8, 64, 256)), "sub", 0, 0, tiled=True)
    return upper_levels(info, whole, got, mine, other, pivot_entries, pivot_inverse)


def solution(mesh):
    cube = ("k", "zl", "xl", "c")
    split = Mesh(mesh.devices.reshape(8, 2, 2, 2, 8), cube + ("sub",))
    return jax.shard_map(
        local,
        mesh=split,
        in_specs=(P(cube, "sub"), P(), P(), P(), P(), P()),
        out_specs=P(cube, "sub"),
        check_vma=False,
    )
```

profile of v0, /device:TPU:416, one launch (start us, length us, event | category | flops | bytes accessed | tf_op | source)
XLA Modules:
  0.0 146.6 jit_solution(5391861030611974468)
XLA Ops:
  0.0 1.0 copy.30
  1.0 3.4 %collective-permute-start = (bf16[256,256]{0,1:T(8,128)(2,1)S(1)}, bf16[256,256]{0,1:T(8,128)(2,1)S(1)}, u32[]{:S(2)}, u32[]{:S(2)}) collective-permute-start(bf16[256,256]{0,1:T(8,128)(2,1)S(1)} %copy.30), channel_id=1, source_target_pairs={{0,16},{1,17},{2,18},{3,19},{4,20},{5,21},{6,22},{7,23},{8,24},{9,... | collective-permute-start | bytes 393224 | tf_op jit(solution)/shard_map/ppermute | solution.py:240
  4.4 2.7 %collective-permute-done = bf16[256,256]{0,1:T(8,128)(2,1)S(1)} collective-permute-done((bf16[256,256]{0,1:T(8,128)(2,1)S(1)}, bf16[256,256]{0,1:T(8,128)(2,1)S(1)}, u32[]{:S(2)}, u32[]{:S(2)}) %collective-permute-start) | collective-permute-done | bytes 131104 | tf_op jit(solution)/shard_map/ppermute | solution.py:240
  7.2 1.3 collective-permute-start.1
  8.5 5.6 %collective-permute-done.1 = bf16[256,256]{0,1:T(8,128)(2,1)S(1)} collective-permute-done((bf16[256,256]{0,1:T(8,128)(2,1)S(1)}, bf16[256,256]{0,1:T(8,128)(2,1)S(1)}, u32[]{:S(2)}, u32[]{:S(2)}) %collective-permute-start.1) | collective-permute-done | bytes 131104 | tf_op jit(solution)/shard_map/ppermute | solution.py:241
  14.0 1.9 %collective-permute-start.2 = (bf16[256,256]{0,1:T(8,128)(2,1)S(1)}, bf16[256,256]{0,1:T(8,128)(2,1)S(1)}, u32[]{:S(2)}, u32[]{:S(2)}) collective-permute-start(bf16[256,256]{0,1:T(8,128)(2,1)S(1)} %broadcast_select_fusion.1), channel_id=1, source_target_pairs={{0,8},{8,0},{1,9},{9,1},{2,10},{10,2},{3,11},{11,3},{4,12},{12,4},... | collective-permute-start | bytes 393224 | tf_op jit(solution)/shard_map/ppermute | solution.py:242
  16.0 1.3 collective-permute-done.2
  17.4 0.8 broadcast_in_dim.46
  18.2 6.6 %all-to-all-start = ((bf16[8,32,896]{2,1,0:T(8,128)(2,1)}), bf16[8,32,896]{2,1,0:T(8,128)(2,1)S(1)}, u32[]{:S(2)}, u32[]{:S(2)}) async-start(bf16[8,32,896]{2,1,0:T(8,128)(2,1)} %broadcast_in_dim.46), calls=%async_computation | async-start | bytes 917504 | tf_op jit(solution)/shard_map/all_to_all | solution.py:256
  25.1 10.9 %all-to-all-done = bf16[8,32,896]{2,1,0:T(8,128)(2,1)S(1)} async-done(((bf16[8,32,896]{2,1,0:T(8,128)(2,1)}), bf16[8,32,896]{2,1,0:T(8,128)(2,1)S(1)}, u32[]{:S(2)}, u32[]{:S(2)}) %all-to-all-start) | async-done | bytes 458784 | tf_op jit(solution)/shard_map/all_to_all | solution.py:256
  37.6 3.4 %collective-permute-start.3 = (bf16[320,256]{1,0:T(8,128)(2,1)S(1)}, bf16[320,256]{1,0:T(8,128)(2,1)S(1)}, u32[]{:S(2)}, u32[]{:S(2)}) collective-permute-start(bf16[320,256]{1,0:T(8,128)(2,1)S(1)} %pad_maximum_fusion.1), channel_id=1, source_target_pairs={{0,64},{64,128},{128,192},{192,256},{256,320},{320,384},{384,448},... | collective-permute-start | bytes 491528 | tf_op jit(solution)/shard_map/ppermute | solution.py:227
  41.0 4.6 %collective-permute-start.4 = (bf16[320,256]{1,0:T(8,128)(2,1)S(1)}, bf16[320,256]{1,0:T(8,128)(2,1)S(1)}, u32[]{:S(2)}, u32[]{:S(2)}) collective-permute-start(bf16[320,256]{1,0:T(8,128)(2,1)S(1)} %pad_maximum_fusion.1), channel_id=1, source_target_pairs={{0,448},{64,0},{128,64},{192,128},{256,192},{320,256},{384,320},{4... | collective-permute-start | bytes 491528 | tf_op jit(solution)/shard_map/ppermute | solution.py:230
  45.8 3.5 %collective-permute-done.3 = bf16[320,256]{1,0:T(8,128)(2,1)S(1)} collective-permute-done((bf16[320,256]{1,0:T(8,128)(2,1)S(1)}, bf16[320,256]{1,0:T(8,128)(2,1)S(1)}, u32[]{:S(2)}, u32[]{:S(2)}) %collective-permute-start.3) | collective-permute-done | bytes 163872 | tf_op jit(solution)/shard_map/ppermute | solution.py:227
  49.3 2.2 %collective-permute-start.5 = (bf16[320,256]{1,0:T(8,128)(2,1)S(1)}, bf16[320,256]{1,0:T(8,128)(2,1)S(1)}, u32[]{:S(2)}, u32[]{:S(2)}) collective-permute-start(bf16[320,256]{1,0:T(8,128)(2,1)S(1)} %collective-permute-done.3), channel_id=1, source_target_pairs={{0,64},{64,128},{128,192},{192,256},{256,320},{320,384},{384,448},... | collective-permute-start | bytes 491528 | tf_op jit(solution)/shard_map/ppermute | solution.py:227
  51.5 5.8 %collective-permute-start.6 = (bf16[320,256]{1,0:T(8,128)(2,1)S(1)}, bf16[320,256]{1,0:T(8,128)(2,1)S(1)}, u32[]{:S(2)}, u32[]{:S(2)}) collective-permute-start(bf16[320,256]{1,0:T(8,128)(2,1)S(1)} %collective-permute-done.4), channel_id=1, source_target_pairs={{0,448},{64,0},{128,64},{192,128},{256,192},{320,256},{384,320},{4... | collective-permute-start | bytes 491528 | tf_op jit(solution)/shard_map/ppermute | solution.py:230
  57.4 2.0 %collective-permute-done.5 = bf16[320,256]{1,0:T(8,128)(2,1)S(1)} collective-permute-done((bf16[320,256]{1,0:T(8,128)(2,1)S(1)}, bf16[320,256]{1,0:T(8,128)(2,1)S(1)}, u32[]{:S(2)}, u32[]{:S(2)}) %collective-permute-start.5) | collective-permute-done | bytes 163872 | tf_op jit(solution)/shard_map/ppermute | solution.py:227
  59.3 1.9 %collective-permute-start.7 = (bf16[320,256]{1,0:T(8,128)(2,1)S(1)}, bf16[320,256]{1,0:T(8,128)(2,1)S(1)}, u32[]{:S(2)}, u32[]{:S(2)}) collective-permute-start(bf16[320,256]{1,0:T(8,128)(2,1)S(1)} %collective-permute-done.5), channel_id=1, source_target_pairs={{0,64},{64,128},{128,192},{192,256},{256,320},{320,384},{384,448},... | collective-permute-start | bytes 491528 | tf_op jit(solution)/shard_map/ppermute | solution.py:227
  61.2 2.1 %collective-permute-done.6 = bf16[320,256]{1,0:T(8,128)(2,1)S(1)} collective-permute-done((bf16[320,256]{1,0:T(8,128)(2,1)S(1)}, bf16[320,256]{1,0:T(8,128)(2,1)S(1)}, u32[]{:S(2)}, u32[]{:S(2)}) %collective-permute-start.6) | collective-permute-done | bytes 163872 | tf_op jit(solution)/shard_map/ppermute | solution.py:230
  63.4 6.5 %collective-permute-start.8 = (bf16[320,256]{1,0:T(8,128)(2,1)S(1)}, bf16[320,256]{1,0:T(8,128)(2,1)S(1)}, u32[]{:S(2)}, u32[]{:S(2)}) collective-permute-start(bf16[320,256]{1,0:T(8,128)(2,1)S(1)} %collective-permute-done.6), channel_id=1, source_target_pairs={{0,448},{64,0},{128,64},{192,128},{256,192},{320,256},{384,320},{4... | collective-permute-start | bytes 491528 | tf_op jit(solution)/shard_map/ppermute | solution.py:230
  69.9 0.3 collective-permute-done.7
  70.2 1.9 %collective-permute-start.9 = (bf16[320,256]{1,0:T(8,128)(2,1)S(1)}, bf16[320,256]{1,0:T(8,128)(2,1)S(1)}, u32[]{:S(2)}, u32[]{:S(2)}) collective-permute-start(bf16[320,256]{1,0:T(8,128)(2,1)S(1)} %collective-permute-done.7), channel_id=1, source_target_pairs={{0,64},{64,128},{128,192},{192,256},{256,320},{320,384},{384,448},... | collective-permute-start | bytes 491528 | tf_op jit(solution)/shard_map/ppermute | solution.py:227
  72.1 1.8 %collective-permute-done.8 = bf16[320,256]{1,0:T(8,128)(2,1)S(1)} collective-permute-done((bf16[320,256]{1,0:T(8,128)(2,1)S(1)}, bf16[320,256]{1,0:T(8,128)(2,1)S(1)}, u32[]{:S(2)}, u32[]{:S(2)}) %collective-permute-start.8) | collective-permute-done | bytes 163872 | tf_op jit(solution)/shard_map/ppermute | solution.py:230
  73.9 6.9 %collective-permute-done.9 = bf16[320,256]{1,0:T(8,128)(2,1)S(1)} collective-permute-done((bf16[320,256]{1,0:T(8,128)(2,1)S(1)}, bf16[320,256]{1,0:T(8,128)(2,1)S(1)}, u32[]{:S(2)}, u32[]{:S(2)}) %collective-permute-start.9) | collective-permute-done | bytes 163872 | tf_op jit(solution)/shard_map/ppermute | solution.py:227
  80.9 0.9 broadcast_in_dim.56
  81.7 4.6 %all-to-all-start.2 = ((bf16[4,8,32,256]{3,2,1,0:T(8,128)(2,1)}), bf16[4,8,32,256]{3,2,1,0:T(8,128)(2,1)S(1)}, u32[]{:S(2)}, u32[]{:S(2)}) async-start(bf16[4,8,32,256]{3,2,1,0:T(8,128)(2,1)} %broadcast_in_dim.56), calls=%async_computation.2 | async-start | bytes 1048576 | tf_op jit(solution)/shard_map/all_to_all | solution.py:288
  86.3 7.1 %all-to-all-done.2.mine = bf16[4,8,32,256]{3,2,1,0:T(8,128)(2,1)S(1)} async-done(((bf16[4,8,32,256]{3,2,1,0:T(8,128)(2,1)}), bf16[4,8,32,256]{3,2,1,0:T(8,128)(2,1)S(1)}, u32[]{:S(2)}, u32[]{:S(2)}) %all-to-all-start.2) | async-done | bytes 524320 | tf_op jit(solution)/shard_map/all_to_all | solution.py:288
  93.5 1.6 %broadcast_in_dim.55 = bf16[8,8,64,256]{3,2,1,0:T(8,128)(2,1)} broadcast(bf16[8,64,256]{2,1,0:T(8,128)(2,1)S(1)} %pad_maximum_fusion), dimensions={1,2,3} | broadcast | bytes 2359296 | tf_op jit(solution)/shard_map/broadcast_in_dim | solution.py:293
  95.1 6.2 %all-to-all-start.1 = ((bf16[8,8,64,256]{3,2,1,0:T(8,128)(2,1)}), bf16[8,8,64,256]{3,2,1,0:T(8,128)(2,1)}, u32[]{:S(2)}, u32[]{:S(2)}) async-start(bf16[8,8,64,256]{3,2,1,0:T(8,128)(2,1)} %broadcast_in_dim.55), calls=%async_computation.1 | async-start | bytes 4194304 | tf_op jit(solution)/shard_map/all_to_all | solution.py:293
  101.2 2.1 %collective-permute-start.10 = (bf16[4,8,32,256]{3,2,1,0:T(8,128)(2,1)S(1)}, bf16[4,8,32,256]{3,2,1,0:T(8,128)(2,1)S(1)}, u32[]{:S(2)}, u32[]{:S(2)}) collective-permute-start(bf16[4,8,32,256]{3,2,1,0:T(8,128)(2,1)S(1)} %all-to-all-done.2.mine), channel_id=1, source_target_pairs={{0,8},{8,0},{1,9},{9,1},{2,10},{10,2},{3,11},{11,3},{4,12},{12,4},... | collective-permute-start | bytes 1572872 | tf_op jit(solution)/shard_map/ppermute | solution.py:291
  103.7 26.3 %all-to-all-done.1.got = bf16[8,8,64,256]{3,2,1,0:T(8,128)(2,1)} async-done(((bf16[8,8,64,256]{3,2,1,0:T(8,128)(2,1)}), bf16[8,8,64,256]{3,2,1,0:T(8,128)(2,1)}, u32[]{:S(2)}, u32[]{:S(2)}) %all-to-all-start.1) | async-done | bytes 2097184 | tf_op jit(solution)/shard_map/all_to_all | solution.py:293
  130.0 1.2 copy-done.1
  131.2 15.4 %upper_levels.1 = bf16[256,2048]{1,0:T(8,128)(2,1)} custom-call(s32[359]{0:T(512)S(1)} %concatenate.27.info, bf16[8,320,256]{2,1,0:T(8,128)(2,1)S(1)} %bitcast_dynamic-update-slice_fusion.whole, bf16[8,8,64,256]{3,2,1,0:T(8,128)(2,1)} %all-to-all-done.1.got, bf16[4,8,32,256]{3,2,1,0:T(8,128)(2,1)S(1)} %all-to-all-done.2.mine, ...), custom_call_target="tpu_custom_call" | custom-call | tf_op jit(solution)/shard_map/upper_levels/pallas_call | solution.py:202
  (52 shorter events, 2.5 us)
Async XLA Ops:
  1.0 6.1 %collective-permute-start = (bf16[256,256]{0,1:T(8,128)(2,1)S(1)}, bf16[256,256]{0,1:T(8,128)(2,1)S(1)}, u32[]{:S(2)}, u32[]{:S(2)}) collective-permute-start(bf16[256,256]{0,1:T(8,128)(2,1)S(1)} %copy.30), channel_id=1, source_target_pairs={{0,16},{1,17},{2,18},{3,19},{4,20},{5,21},{6,22},{7,23},{8,24},{9,... | collective-permute-start | bytes 393224 | tf_op jit(solution)/shard_map/ppermute | solution.py:240
  7.2 6.9 %collective-permute-start.1 = (bf16[256,256]{0,1:T(8,128)(2,1)S(1)}, bf16[256,256]{0,1:T(8,128)(2,1)S(1)}, u32[]{:S(2)}, u32[]{:S(2)}) collective-permute-start(bf16[256,256]{0,1:T(8,128)(2,1)S(1)} %broadcast_select_fusion), channel_id=1, source_target_pairs={{0,32},{1,33},{2,34},{3,35},{4,36},{5,37},{6,38},{7,39},{8,40},{9,... | collective-permute-start | bytes 393224 | tf_op jit(solution)/shard_map/ppermute | solution.py:241
  14.0 3.2 %collective-permute-start.2 = (bf16[256,256]{0,1:T(8,128)(2,1)S(1)}, bf16[256,256]{0,1:T(8,128)(2,1)S(1)}, u32[]{:S(2)}, u32[]{:S(2)}) collective-permute-start(bf16[256,256]{0,1:T(8,128)(2,1)S(1)} %broadcast_select_fusion.1), channel_id=1, source_target_pairs={{0,8},{8,0},{1,9},{9,1},{2,10},{10,2},{3,11},{11,3},{4,12},{12,4},... | collective-permute-start | bytes 393224 | tf_op jit(solution)/shard_map/ppermute | solution.py:242
  18.2 17.8 %all-to-all-start = ((bf16[8,32,896]{2,1,0:T(8,128)(2,1)}), bf16[8,32,896]{2,1,0:T(8,128)(2,1)S(1)}, u32[]{:S(2)}, u32[]{:S(2)}) async-start(bf16[8,32,896]{2,1,0:T(8,128)(2,1)} %broadcast_in_dim.46), calls=%async_computation | async-start | bytes 917504 | tf_op jit(solution)/shard_map/all_to_all | solution.py:256
  24.9 11.2 %copy-start = (bf16[15,2,128,128]{3,2,1,0:T(8,128)(2,1)S(1)}, bf16[15,2,128,128]{3,2,1,0:T(8,128)(2,1)}, u32[]{:S(2)}) copy-start(bf16[15,2,128,128]{3,2,1,0:T(8,128)(2,1)} %inverses.1) | copy-start | bytes 2949124
  37.6 11.7 %collective-permute-start.3 = (bf16[320,256]{1,0:T(8,128)(2,1)S(1)}, bf16[320,256]{1,0:T(8,128)(2,1)S(1)}, u32[]{:S(2)}, u32[]{:S(2)}) collective-permute-start(bf16[320,256]{1,0:T(8,128)(2,1)S(1)} %pad_maximum_fusion.1), channel_id=1, source_target_pairs={{0,64},{64,128},{128,192},{192,256},{256,320},{320,384},{384,448},... | collective-permute-start | bytes 491528 | tf_op jit(solution)/shard_map/ppermute | solution.py:227
  41.0 10.5 %collective-permute-start.4 = (bf16[320,256]{1,0:T(8,128)(2,1)S(1)}, bf16[320,256]{1,0:T(8,128)(2,1)S(1)}, u32[]{:S(2)}, u32[]{:S(2)}) collective-permute-start(bf16[320,256]{1,0:T(8,128)(2,1)S(1)} %pad_maximum_fusion.1), channel_id=1, source_target_pairs={{0,448},{64,0},{128,64},{192,128},{256,192},{320,256},{384,320},{4... | collective-permute-start | bytes 491528 | tf_op jit(solution)/shard_map/ppermute | solution.py:230
  49.3 10.0 %collective-permute-start.5 = (bf16[320,256]{1,0:T(8,128)(2,1)S(1)}, bf16[320,256]{1,0:T(8,128)(2,1)S(1)}, u32[]{:S(2)}, u32[]{:S(2)}) collective-permute-start(bf16[320,256]{1,0:T(8,128)(2,1)S(1)} %collective-permute-done.3), channel_id=1, source_target_pairs={{0,64},{64,128},{128,192},{192,256},{256,320},{320,384},{384,448},... | collective-permute-start | bytes 491528 | tf_op jit(solution)/shard_map/ppermute | solution.py:227
  51.5 11.9 %collective-permute-start.6 = (bf16[320,256]{1,0:T(8,128)(2,1)S(1)}, bf16[320,256]{1,0:T(8,128)(2,1)S(1)}, u32[]{:S(2)}, u32[]{:S(2)}) collective-permute-start(bf16[320,256]{1,0:T(8,128)(2,1)S(1)} %collective-permute-done.4), channel_id=1, source_target_pairs={{0,448},{64,0},{128,64},{192,128},{256,192},{320,256},{384,320},{4... | collective-permute-start | bytes 491528 | tf_op jit(solution)/shard_map/ppermute | solution.py:230
  59.3 10.9 %collective-permute-start.7 = (bf16[320,256]{1,0:T(8,128)(2,1)S(1)}, bf16[320,256]{1,0:T(8,128)(2,1)S(1)}, u32[]{:S(2)}, u32[]{:S(2)}) collective-permute-start(bf16[320,256]{1,0:T(8,128)(2,1)S(1)} %collective-permute-done.5), channel_id=1, source_target_pairs={{0,64},{64,128},{128,192},{192,256},{256,320},{320,384},{384,448},... | collective-permute-start | bytes 491528 | tf_op jit(solution)/shard_map/ppermute | solution.py:227
  63.4 10.5 %collective-permute-start.8 = (bf16[320,256]{1,0:T(8,128)(2,1)S(1)}, bf16[320,256]{1,0:T(8,128)(2,1)S(1)}, u32[]{:S(2)}, u32[]{:S(2)}) collective-permute-start(bf16[320,256]{1,0:T(8,128)(2,1)S(1)} %collective-permute-done.6), channel_id=1, source_target_pairs={{0,448},{64,0},{128,64},{192,128},{256,192},{320,256},{384,320},{4... | collective-permute-start | bytes 491528 | tf_op jit(solution)/shard_map/ppermute | solution.py:230
  70.2 10.6 %collective-permute-start.9 = (bf16[320,256]{1,0:T(8,128)(2,1)S(1)}, bf16[320,256]{1,0:T(8,128)(2,1)S(1)}, u32[]{:S(2)}, u32[]{:S(2)}) collective-permute-start(bf16[320,256]{1,0:T(8,128)(2,1)S(1)} %collective-permute-done.7), channel_id=1, source_target_pairs={{0,64},{64,128},{128,192},{192,256},{256,320},{320,384},{384,448},... | collective-permute-start | bytes 491528 | tf_op jit(solution)/shard_map/ppermute | solution.py:227
  81.7 11.8 %all-to-all-start.2 = ((bf16[4,8,32,256]{3,2,1,0:T(8,128)(2,1)}), bf16[4,8,32,256]{3,2,1,0:T(8,128)(2,1)S(1)}, u32[]{:S(2)}, u32[]{:S(2)}) async-start(bf16[4,8,32,256]{3,2,1,0:T(8,128)(2,1)} %broadcast_in_dim.56), calls=%async_computation.2 | async-start | bytes 1048576 | tf_op jit(solution)/shard_map/all_to_all | solution.py:288
  95.1 8.3 %copy-start.2 = (s32[4,2,14]{2,1,0:T(2,128)S(1)}, s32[4,2,14]{2,1,0:T(2,128)}, u32[]{:S(2)}) copy-start(s32[4,2,14]{2,1,0:T(2,128)} %param.9) | copy-start | bytes 1348
  95.1 8.4 %copy-start.3 = (s32[2,2,30]{2,1,0:T(2,128)S(1)}, s32[2,2,30]{2,1,0:T(2,128)}, u32[]{:S(2)}) copy-start(s32[2,2,30]{2,1,0:T(2,128)} %param.10) | copy-start | bytes 1444
  95.1 8.4 %copy-start.4 = (s32[1,2,62]{2,1,0:T(2,128)S(1)}, s32[1,2,62]{2,1,0:T(2,128)}, u32[]{:S(2)}) copy-start(s32[1,2,62]{2,1,0:T(2,128)} %param.11) | copy-start | bytes 1492
  95.1 34.9 %all-to-all-start.1 = ((bf16[8,8,64,256]{3,2,1,0:T(8,128)(2,1)}), bf16[8,8,64,256]{3,2,1,0:T(8,128)(2,1)}, u32[]{:S(2)}, u32[]{:S(2)}) async-start(bf16[8,8,64,256]{3,2,1,0:T(8,128)(2,1)} %broadcast_in_dim.55), calls=%async_computation.1 | async-start | bytes 4194304 | tf_op jit(solution)/shard_map/all_to_all | solution.py:293
  101.2 28.8 %collective-permute-start.10 = (bf16[4,8,32,256]{3,2,1,0:T(8,128)(2,1)S(1)}, bf16[4,8,32,256]{3,2,1,0:T(8,128)(2,1)S(1)}, u32[]{:S(2)}, u32[]{:S(2)}) collective-permute-start(bf16[4,8,32,256]{3,2,1,0:T(8,128)(2,1)S(1)} %all-to-all-done.2.mine), channel_id=1, source_target_pairs={{0,8},{8,0},{1,9},{9,1},{2,10},{10,2},{3,11},{11,3},{4,12},{12,4},... | collective-permute-start | bytes 1572872 | tf_op jit(solution)/shard_map/ppermute | solution.py:291
  130.0 1.2 copy-start.1
where the time goes:
time: 147 us
  waiting for transfers between devices  70.4 us (48%)
  starting transfers between devices  52.3 us (36%)
  Pallas kernels  15.4 us (10%)
  local copies, waits for them, and re-layouts  6.37 us (4%)
    all_to_all x1, waiting for transfers between devices, local(): lax.all_to_all(jnp.broadcast_to(piece[None], (8, 8, 64, 256)), 'sub', 0,...  26.3 us
    ppermute x3, starting transfers between devices, gather_ring(): behind = lax.ppermute(behind, 'k', down)  16.8 us
    pallas_call x1, Pallas kernels, upper_levels(): pl.pallas_call(upper_kernel, out_shape=jax.ShapeDtypeStruct((256, 2048),...  15.4 us
    ppermute x4, waiting for transfers between devices, gather_ring(): ahead = lax.ppermute(ahead, 'k', up)  12.6 us
    all_to_all x1, waiting for transfers between devices, leaf_stage(): lax.all_to_all(jnp.broadcast_to(piece[None], (8,) + piece.shape), 'sub',...  10.9 us
    ppermute x4, starting transfers between devices, gather_ring(): ahead = lax.ppermute(ahead, 'k', up)  9.35 us
    all_to_all x1, waiting for transfers between devices, local(): lax.all_to_all(jnp.broadcast_to(whole[None, :, 288:], (4, 8, 32, 256)), (...  7.14 us
    all_to_all x1, starting transfers between devices, leaf_stage(): lax.all_to_all(jnp.broadcast_to(piece[None], (8,) + piece.shape), 'sub',...  6.64 us
  transfers between devices with their start and end apart: 14, of which 12 were waited for; matrix products, arithmetic and copies ran while one was open for 1% of the time, Pallas kernels for 0%

commit v1 on v0

--- a/solution.py
+++ b/solution.py
@@ -31,7 +31,7 @@
 
 
 def upper_kernel(
-    info, whole, got, mine, other, pivots, inverses, out,
+    info, whole, got, near, other, pivots, inverses, out,
     z_one, z_two, z_top, y_one, y_two, y_top, t_one, t_two, own_one, own_two, core_one, core_two,
 ):
     p, s, c = info[0], info[1], info[2]
@@ -67,12 +67,16 @@
             parts.append(jnp.where(spot >= 0, part, jnp.zeros_like(part)))
         return jnp.concatenate(parts, 1)
 
+    def stacked(front, lanes):
+        return jnp.concatenate([got[sub, front, :, lanes] for sub in range(8)], 0)
+
     def leaf_own(front, q):
-        stacked = [got[sub, front, 16 * q : 16 * q + 16, :] for sub in range(8)]
-        return leaf_slots(front, jnp.concatenate(stacked, 0))
+        return leaf_slots(front, stacked(front, slice(256 * q, 256 * q + 256)))
 
     def leaf_core(front):
-        return jnp.concatenate([got[sub, front, 32:64, :] for sub in range(8)], 0)
+        blocks = stacked(front, slice(512, 896))
+        turned = blocks[:, BLOCK : 2 * BLOCK].astype(F32).T.astype(BF16)
+        return blocks[:, : 2 * BLOCK], jnp.concatenate([turned, blocks[:, 2 * BLOCK :]], 1)
 
     for level in (1, 2, 3):
         z_ref, y_ref = z_refs[level], y_refs[level]
@@ -108,9 +112,12 @@
 
                 if level == 1:
                     for block in range(2, 16):
-                        here = (block // 4, kid, pl.ds(16 * (block % 2), 16))
-                        panel = jnp.where(c == block // 2 % 2, mine[here], other[here])
-                        row = leaf_slots(kid, whole[kid, 16 * block : 16 * block + 16, :])
+                        at = slice(16 * (block - 2), 16 * (block - 1))
+                        one, two = near[kid, at, :], other[kid, at, :]
+                        panel = jnp.concatenate(
+                            [jnp.where(c == 0, one, two), jnp.where(c == 0, two, one)], 1
+                        )
+                        row = leaf_slots(kid, whole[kid, at, :])
                         put(block, entry(level, front, child, block - 2), panel, row)
                 else:
                     def step(block, carry):
@@ -136,13 +143,16 @@
                     y_ref[0, 16 * half : 16 * half + 16, :BLOCK] += strip
 
             core_rows = (2, 3, 1) if level < 3 else (1,)
+            if level == 1:
+                kid_own = [[leaf_own(kid, q) for q in range(2)] for kid in kids]
+                kid_core = [leaf_core(kid) for kid in kids]
             zt = []
             for q in range(wanted):
                 parts = []
                 own = jnp.zeros((BLOCK, 256), F32)
                 for child, kid in enumerate(kids):
                     if level == 1:
-                        value = leaf_own(kid, q % 2)
+                        value = kid_own[child][q % 2]
                     else:
                         value = own_refs[level - 1][kid, (q % 2) * BLOCK : (q % 2 + 1) * BLOCK, :]
                     own = own + masked(child, q, value.astype(F32))
@@ -156,7 +166,7 @@
                     value = jnp.zeros((BLOCK, BLOCK), F32)
                     for child, kid in enumerate(kids):
                         if level == 1:
-                            part = leaf_core(kid)[(q % 2) * BLOCK : (q % 2 + 1) * BLOCK]
+                            part = kid_core[child][q % 2]
                         else:
                             part = core_refs[level - 1][kid, (q % 2) * BLOCK : (q % 2 + 1) * BLOCK, :]
                         part = part[:, (r % 2) * BLOCK : (r % 2 + 1) * BLOCK].astype(F32)
@@ -197,7 +207,7 @@
                 t_refs[level][front, at, :] = rest.astype(BF16)
 
 
-def upper_levels(info, whole, got, mine, other, pivots, inverses):
+def upper_levels(info, whole, got, near, other, pivots, inverses):
     vmem = pl.BlockSpec(memory_space=pltpu.VMEM)
     return pl.pallas_call(
         upper_kernel,
@@ -215,27 +225,10 @@
         ],
         compiler_params=pltpu.CompilerParams(vmem_limit_bytes=48 * 2**20),
         name="upper_levels",
-    )(info, whole, got, mine, other, pivots, inverses)
-
-
-def gather_ring(payload, k, count):
-    parts = [(payload, k)]
-    ahead = behind = payload
-    up = [(i, (i + 1) % count) for i in range(count)]
-    down = [(i, (i - 1) % count) for i in range(count)]
-    for step in range(1, count // 2 + 1):
-        ahead = lax.ppermute(ahead, "k", up)
-        parts.append((ahead, (k - step) % count))
-        if step < count // 2:
-            behind = lax.ppermute(behind, "k", down)
-            parts.append((behind, (k + step) % count))
-    whole = jnp.zeros((count,) + payload.shape, payload.dtype)
-    for part, spot in parts:
-        whole = lax.dynamic_update_slice_in_dim(whole, part[None], spot, 0)
-    return whole
-
-
-def leaf_stage(leaf, inverses, zl, xl, c, u, s):
+    )(info, whole, got, near, other, pivots, inverses)
+
+
+def leaf_stage(leaf, inverses, zl, xl, c, s):
     tile = leaf
     spread = jnp.where(xl == 0, tile, lax.ppermute(tile, "xl", [(0, 1)]))
     spread = jnp.where(zl == 0, spread, lax.ppermute(spread, "zl", [(0, 1)]))
@@ -260,17 +253,12 @@
     columns, scaled = panels(first, second, inverses[0], inverses[1], 512)
     core = got[:, :, 640:].reshape(256, 256).astype(F32)
     core = core - dot_tn(columns[:, 640:], scaled[:, 640:])
-    cols = jnp.concatenate([even[BLOCK:], odd[BLOCK:]], 0).T.astype(F32)
-    cols = cols - dot_tn(scaled[:, :256], columns[:, 640:])
+    core = core.astype(BF16)
+    core = jnp.concatenate([core[:BLOCK, :BLOCK], core[:BLOCK, BLOCK:], core[BLOCK:, BLOCK:]], 1)
+    core = lax.dynamic_slice_in_dim(core, 16 * s, 16, 0)
     tile = tile.T.astype(F32) - dot_tn(columns[:, :256], scaled[:, 256:512])
-    return jnp.concatenate(
-        [
-            tile.astype(BF16),
-            lax.dynamic_slice_in_dim(core.astype(BF16), 32 * s, 32, 0),
-            lax.dynamic_slice_in_dim(cols.astype(BF16), 32 * u, 32, 0),
-        ],
-        0,
-    )
+    rest = jnp.concatenate([core[:8, 256:], core[8:, 256:]], 1)
+    return jnp.concatenate([tile[32:].astype(BF16), core[:, :256], rest], 0)
 
 
 def local(leaf_fronts, pivot_entries, pivot_inverse, block_map_one, block_map_two, block_map_top):
@@ -282,16 +270,26 @@
         [jnp.stack([k * 8 + u, s, c]).astype(jnp.int32)] + [table.reshape(-1) for table in maps]
     )
     payload = leaf_stage(
-        leaf_fronts, lax.dynamic_index_in_dim(pivot_inverse, k, 0, keepdims=False), zl, xl, c, u, s
+        leaf_fronts, lax.dynamic_index_in_dim(pivot_inverse, k, 0, keepdims=False), zl, xl, c, s
     )
-    whole = gather_ring(payload, k, 8)
-    mine = lax.all_to_all(
-        jnp.broadcast_to(whole[None, :, 288:], (4, 8, 32, 256)), ("zl", "xl"), 0, 0, tiled=True
+    whole = lax.all_gather(payload, "k")
+    rest = jnp.concatenate([whole[:, 240:, :BLOCK], whole[:, 240:, BLOCK:]], 1)
+    piece = jnp.concatenate([whole[:, 96:112], whole[:, 112:128], whole[:, 224:240], rest], 2)
+    got = lax.all_to_all(jnp.broadcast_to(piece[None], (8, 8, 16, 896)), "sub", 0, 0, tiled=True)
+
+    def spread(value, axis, position):
+        return jnp.where(position == 0, value, lax.ppermute(value, axis, [(0, 1)]))
+
+    later = whole[:, :224, BLOCK:]
+    near = jnp.concatenate(
+        [
+            spread(spread(later[:4], "xl", xl), "zl", zl),
+            spread(spread(later[4:], "zl", zl), "xl", xl),
+        ],
+        0,
     )
-    other = lax.ppermute(mine, "c", [(0, 1), (1, 0)])
-    piece = jnp.concatenate([whole[:, 128:160], whole[:, 256:288]], 1)
-    got = lax.all_to_all(jnp.broadcast_to(piece[None], (8, 8, 64, 256)), "sub", 0, 0, tiled=True)
-    return upper_levels(info, whole, got, mine, other, pivot_entries, pivot_inverse)
+    other = lax.ppermute(near, "c", [(0, 1), (1, 0)])
+    return upper_levels(info, whole, got, near, other, pivot_entries, pivot_inverse)
 
 
 def solution(mesh):

time: 147 us -> 135 us (0.918)
  the two profiles are of different devices: /device:TPU:416 before, /device:TPU:7 now
where the time goes in v1:
time: 135 us
  starting transfers between devices  40.3 us (30%)
  blocking collectives  34.9 us (26%)
  waiting for transfers between devices  33.8 us (25%)
  Pallas kernels  14.9 us (11%)
  local copies, waits for them, and re-layouts  7.33 us (5%)
  matrix products  2.66 us (2%)
    all_gather x1, blocking collectives, local(): whole = lax.all_gather(payload, 'k')  34.9 us
    ppermute x4, waiting for transfers between devices, spread(): return jnp.where(position == 0, value, lax.ppermute(value, axis, [(0, 1)]))  17.9 us
    pallas_call x1, Pallas kernels, upper_levels(): pl.pallas_call(upper_kernel, out_shape=jax.ShapeDtypeStruct((256, 2048),...  14.9 us
    ppermute x1, starting transfers between devices, local(): other = lax.ppermute(near, 'c', [(0, 1), (1, 0)])  9.21 us
    ppermute x4, starting transfers between devices, spread(): return jnp.where(position == 0, value, lax.ppermute(value, axis, [(0, 1)]))  8.25 us
    all_to_all x1, waiting for transfers between devices, leaf_stage(): lax.all_to_all(jnp.broadcast_to(piece[None], (8,) + piece.shape), 'sub',...  7.67 us
    all_to_all x1, starting transfers between devices, leaf_stage(): lax.all_to_all(jnp.broadcast_to(piece[None], (8,) + piece.shape), 'sub',...  6.87 us
    all_to_all x1, starting transfers between devices, local(): lax.all_to_all(jnp.broadcast_to(piece[None], (8, 8, 16, 896)), 'sub', 0,...  6.87 us
  transfers between devices with their start and end apart: 10, of which 6 were waited for; matrix products, arithmetic and copies ran while one was open for 2% of the time, Pallas kernels for 0%

profile of v1, /device:TPU:7, one launch (start us, length us, event | category | flops | bytes accessed | tf_op | source)
XLA Modules:
  0.0 134.7 jit_solution(17337023494629590763)
XLA Ops:
  0.0 1.3 collective-permute-start
  1.3 5.2 %collective-permute-done = bf16[256,256]{1,0:T(8,128)(2,1)S(1)} collective-permute-done((bf16[256,256]{1,0:T(8,128)(2,1)}, bf16[256,256]{1,0:T(8,128)(2,1)S(1)}, u32[]{:S(2)}, u32[]{:S(2)}) %collective-permute-start) | collective-permute-done | bytes 131104 | tf_op jit(solution)/shard_map/ppermute | solution.py:233
  6.5 3.5 %collective-permute-start.1 = (bf16[256,256]{1,0:T(8,128)(2,1)S(1)}, bf16[256,256]{1,0:T(8,128)(2,1)S(1)}, u32[]{:S(2)}, u32[]{:S(2)}) collective-permute-start(bf16[256,256]{1,0:T(8,128)(2,1)S(1)} %broadcast_select_fusion.4), channel_id=1, source_target_pairs={{0,32},{1,33},{2,34},{3,35},{4,36},{5,37},{6,38},{7,39},{8,40},{9,... | collective-permute-start | bytes 393224 | tf_op jit(solution)/shard_map/ppermute | solution.py:234
  10.0 1.0 copy.14
  11.1 0.9 collective-permute-done.1
  12.0 4.3 %collective-permute-start.2 = (bf16[256,256]{1,0:T(8,128)(2,1)S(1)}, bf16[256,256]{1,0:T(8,128)(2,1)S(1)}, u32[]{:S(2)}, u32[]{:S(2)}) collective-permute-start(bf16[256,256]{1,0:T(8,128)(2,1)S(1)} %broadcast_select_fusion.5), channel_id=1, source_target_pairs={{0,8},{8,0},{1,9},{9,1},{2,10},{10,2},{3,11},{11,3},{4,12},{12,4},... | collective-permute-start | bytes 393224 | tf_op jit(solution)/shard_map/ppermute | solution.py:235
  16.3 1.0 collective-permute-done.2
  17.5 0.1 copy.18
  17.6 0.1 copy.19
  17.7 0.1 copy.20
  17.8 0.8 broadcast_in_dim.4
  18.6 6.9 %all-to-all-start = ((bf16[8,32,896]{2,1,0:T(8,128)(2,1)}), bf16[8,32,896]{2,1,0:T(8,128)(2,1)S(1)}, u32[]{:S(2)}, u32[]{:S(2)}) async-start(bf16[8,32,896]{2,1,0:T(8,128)(2,1)} %broadcast_in_dim.4), calls=%async_computation | async-start | bytes 917504 | tf_op jit(solution)/shard_map/all_to_all | solution.py:249
  25.6 7.7 %all-to-all-done = bf16[8,32,896]{2,1,0:T(8,128)(2,1)S(1)} async-done(((bf16[8,32,896]{2,1,0:T(8,128)(2,1)}), bf16[8,32,896]{2,1,0:T(8,128)(2,1)S(1)}, u32[]{:S(2)}, u32[]{:S(2)}) %all-to-all-start) | async-done | bytes 458784 | tf_op jit(solution)/shard_map/all_to_all | solution.py:249
  33.3 1.0 convolution_convert_fusion.1
  34.3 0.2 subtract_convert_fusion
  34.6 1.0 convolution_convert_fusion
  35.5 0.2 fusion
  35.9 0.2 fusion.7
  36.1 34.9 %all-gather = bf16[1984,256]{1,0:T(8,128)(2,1)S(1)} all-gather(bf16[248,256]{1,0:T(8,128)(2,1)S(1)} %maximum_maximum_fusion.1), channel_id=2, replica_groups=mesh['k'=8,'zl'=2,'xl'=2,'c'=2,'sub'=8] {'k'}, dimensions={0}, use_global_device_ids=true | all-gather | bytes 1142784 | tf_op jit(solution)/shard_map/all_gather | solution.py:275
  71.1 0.8 fusion.26
  71.9 1.3 collective-permute-start.3
  73.2 4.4 %collective-permute-start.5 = (bf16[4,224,128]{2,1,0:T(8,128)(2,1)S(1)}, bf16[4,224,128]{2,1,0:T(8,128)(2,1)S(1)}, u32[]{:S(2)}, u32[]{:S(2)}) collective-permute-start(bf16[4,224,128]{2,1,0:T(8,128)(2,1)S(1)} %get-tuple-element.8), channel_id=1, source_target_pairs={{0,32},{1,33},{2,34},{3,35},{4,36},{5,37},{6,38},{7,39},{8,40},{9,... | collective-permute-start | bytes 688136 | tf_op jit(solution)/shard_map/ppermute | solution.py:281
  77.6 1.4 %broadcast_in_dim.5 = bf16[8,8,16,896]{3,2,1,0:T(8,128)(2,1)} broadcast(bf16[8,16,896]{2,1,0:T(8,128)(2,1)S(1)} %maximum_maximum_fusion), dimensions={1,2,3} | broadcast | bytes 2064384 | tf_op jit(solution)/shard_map/broadcast_in_dim | solution.py:278
  79.0 6.9 %all-to-all-start.1 = ((bf16[8,8,16,896]{3,2,1,0:T(8,128)(2,1)}), bf16[8,8,16,896]{3,2,1,0:T(8,128)(2,1)S(1)}, u32[]{:S(2)}, u32[]{:S(2)}) async-start(bf16[8,8,16,896]{3,2,1,0:T(8,128)(2,1)} %broadcast_in_dim.5), calls=%async_computation.1 | async-start | bytes 3670016 | tf_op jit(solution)/shard_map/all_to_all | solution.py:278
  85.9 1.3 collective-permute-start.6
  87.2 1.3 collective-permute-start.4
  88.6 17.9 %collective-permute-done.6 = bf16[4,224,128]{2,1,0:T(8,128)(2,1)S(1)} collective-permute-done((bf16[4,224,128]{2,1,0:T(8,128)(2,1)S(1)}, bf16[4,224,128]{2,1,0:T(8,128)(2,1)S(1)}, u32[]{:S(2)}, u32[]{:S(2)}) %collective-permute-start.6) | collective-permute-done | bytes 229408 | tf_op jit(solution)/shard_map/ppermute | solution.py:281
  106.6 9.2 %collective-permute-start.7 = (bf16[8,224,128]{2,1,0:T(8,128)(2,1)S(1)}, bf16[8,224,128]{2,1,0:T(8,128)(2,1)}, u32[]{:S(2)}, u32[]{:S(2)}) collective-permute-start(bf16[8,224,128]{2,1,0:T(8,128)(2,1)S(1)} %pad_maximum_fusion.near), channel_id=1, source_target_pairs={{0,8},{8,0},{1,9},{9,1},{2,10},{10,2},{3,11},{11,3},{4,12},{12,4},... | collective-permute-start | bytes 1376264 | tf_op jit(solution)/shard_map/ppermute | solution.py:291
  116.2 1.2 collective-permute-done.7.other
  117.4 1.2 copy-done
  118.6 1.2 copy-done.1
  119.8 14.9 %upper_levels.1 = bf16[256,2048]{1,0:T(8,128)(2,1)} custom-call(s32[359]{0:T(512)S(1)} %concatenate.37.info, bf16[8,248,256]{2,1,0:T(8,128)(2,1)S(1)} %bitcast.29, bf16[8,8,16,896]{3,2,1,0:T(8,128)(2,1)S(1)} %all-to-all-done.1.got, bf16[8,224,128]{2,1,0:T(8,128)(2,1)S(1)} %pad_maximum_fusion.near, bf16[8,224,128]{2,1,0:T(8,128)(2,1)} %collective-permute-done.7.other, ...), custom_call_target="tpu_custom_call" | custom-call | tf_op jit(solution)/shard_map/upper_levels/pallas_call | solution.py:212
  (48 shorter events, 1.0 us)
Async XLA Ops:
  0.0 6.5 %collective-permute-start = (bf16[256,256]{1,0:T(8,128)(2,1)}, bf16[256,256]{1,0:T(8,128)(2,1)S(1)}, u32[]{:S(2)}, u32[]{:S(2)}) collective-permute-start(bf16[256,256]{1,0:T(8,128)(2,1)} %param.6), channel_id=1, source_target_pairs={{0,16},{1,17},{2,18},{3,19},{4,20},{5,21},{6,22},{7,23},{8,24},{9,... | collective-permute-start | bytes 393224 | tf_op jit(solution)/shard_map/ppermute | solution.py:233
  6.5 5.5 %collective-permute-start.1 = (bf16[256,256]{1,0:T(8,128)(2,1)S(1)}, bf16[256,256]{1,0:T(8,128)(2,1)S(1)}, u32[]{:S(2)}, u32[]{:S(2)}) collective-permute-start(bf16[256,256]{1,0:T(8,128)(2,1)S(1)} %broadcast_select_fusion.4), channel_id=1, source_target_pairs={{0,32},{1,33},{2,34},{3,35},{4,36},{5,37},{6,38},{7,39},{8,40},{9,... | collective-permute-start | bytes 393224 | tf_op jit(solution)/shard_map/ppermute | solution.py:234
  12.0 5.3 %collective-permute-start.2 = (bf16[256,256]{1,0:T(8,128)(2,1)S(1)}, bf16[256,256]{1,0:T(8,128)(2,1)S(1)}, u32[]{:S(2)}, u32[]{:S(2)}) collective-permute-start(bf16[256,256]{1,0:T(8,128)(2,1)S(1)} %broadcast_select_fusion.5), channel_id=1, source_target_pairs={{0,8},{8,0},{1,9},{9,1},{2,10},{10,2},{3,11},{11,3},{4,12},{12,4},... | collective-permute-start | bytes 393224 | tf_op jit(solution)/shard_map/ppermute | solution.py:235
  18.6 14.6 %all-to-all-start = ((bf16[8,32,896]{2,1,0:T(8,128)(2,1)}), bf16[8,32,896]{2,1,0:T(8,128)(2,1)S(1)}, u32[]{:S(2)}, u32[]{:S(2)}) async-start(bf16[8,32,896]{2,1,0:T(8,128)(2,1)} %broadcast_in_dim.4), calls=%async_computation | async-start | bytes 917504 | tf_op jit(solution)/shard_map/all_to_all | solution.py:249
  71.9 14.0 %collective-permute-start.3 = (bf16[4,224,128]{2,1,0:T(8,128)(2,1)}, bf16[4,224,128]{2,1,0:T(8,128)(2,1)S(1)}, u32[]{:S(2)}, u32[]{:S(2)}) collective-permute-start(bf16[4,224,128]{2,1,0:T(8,128)(2,1)} %get-tuple-element.7), channel_id=1, source_target_pairs={{0,16},{1,17},{2,18},{3,19},{4,20},{5,21},{6,22},{7,23},{8,24},{9,... | collective-permute-start | bytes 688136 | tf_op jit(solution)/shard_map/ppermute | solution.py:281
  73.2 12.7 %collective-permute-start.5 = (bf16[4,224,128]{2,1,0:T(8,128)(2,1)S(1)}, bf16[4,224,128]{2,1,0:T(8,128)(2,1)S(1)}, u32[]{:S(2)}, u32[]{:S(2)}) collective-permute-start(bf16[4,224,128]{2,1,0:T(8,128)(2,1)S(1)} %get-tuple-element.8), channel_id=1, source_target_pairs={{0,32},{1,33},{2,34},{3,35},{4,36},{5,37},{6,38},{7,39},{8,40},{9,... | collective-permute-start | bytes 688136 | tf_op jit(solution)/shard_map/ppermute | solution.py:281
  79.0 38.4 %all-to-all-start.1 = ((bf16[8,8,16,896]{3,2,1,0:T(8,128)(2,1)}), bf16[8,8,16,896]{3,2,1,0:T(8,128)(2,1)S(1)}, u32[]{:S(2)}, u32[]{:S(2)}) async-start(bf16[8,8,16,896]{3,2,1,0:T(8,128)(2,1)} %broadcast_in_dim.5), calls=%async_computation.1 | async-start | bytes 3670016 | tf_op jit(solution)/shard_map/all_to_all | solution.py:278
  85.9 30.0 %copy-start.2 = (s32[4,2,14]{2,1,0:T(2,128)S(1)}, s32[4,2,14]{2,1,0:T(2,128)}, u32[]{:S(2)}) copy-start(s32[4,2,14]{2,1,0:T(2,128)} %param.9) | copy-start | bytes 1348
  85.9 30.1 %copy-start.3 = (s32[2,2,30]{2,1,0:T(2,128)S(1)}, s32[2,2,30]{2,1,0:T(2,128)}, u32[]{:S(2)}) copy-start(s32[2,2,30]{2,1,0:T(2,128)} %param.10) | copy-start | bytes 1444
  85.9 30.1 %copy-start.4 = (s32[1,2,62]{2,1,0:T(2,128)S(1)}, s32[1,2,62]{2,1,0:T(2,128)}, u32[]{:S(2)}) copy-start(s32[1,2,62]{2,1,0:T(2,128)} %param.11) | copy-start | bytes 1492
  85.9 20.5 %collective-permute-start.6 = (bf16[4,224,128]{2,1,0:T(8,128)(2,1)S(1)}, bf16[4,224,128]{2,1,0:T(8,128)(2,1)S(1)}, u32[]{:S(2)}, u32[]{:S(2)}) collective-permute-start(bf16[4,224,128]{2,1,0:T(8,128)(2,1)S(1)} %get-tuple-element.6), channel_id=1, source_target_pairs={{0,16},{1,17},{2,18},{3,19},{4,20},{5,21},{6,22},{7,23},{8,24},{9,... | collective-permute-start | bytes 688136 | tf_op jit(solution)/shard_map/ppermute | solution.py:281
  87.2 19.3 %collective-permute-start.4 = (bf16[4,224,128]{2,1,0:T(8,128)(2,1)S(1)}, bf16[4,224,128]{2,1,0:T(8,128)(2,1)S(1)}, u32[]{:S(2)}, u32[]{:S(2)}) collective-permute-start(bf16[4,224,128]{2,1,0:T(8,128)(2,1)S(1)} %get-tuple-element.5), channel_id=1, source_target_pairs={{0,32},{1,33},{2,34},{3,35},{4,36},{5,37},{6,38},{7,39},{8,40},{9,... | collective-permute-start | bytes 688136 | tf_op jit(solution)/shard_map/ppermute | solution.py:281
  106.6 10.8 %collective-permute-start.7 = (bf16[8,224,128]{2,1,0:T(8,128)(2,1)S(1)}, bf16[8,224,128]{2,1,0:T(8,128)(2,1)}, u32[]{:S(2)}, u32[]{:S(2)}) collective-permute-start(bf16[8,224,128]{2,1,0:T(8,128)(2,1)S(1)} %pad_maximum_fusion.near), channel_id=1, source_target_pairs={{0,8},{8,0},{1,9},{9,1},{2,10},{10,2},{3,11},{11,3},{4,12},{12,4},... | collective-permute-start | bytes 1376264 | tf_op jit(solution)/shard_map/ppermute | solution.py:291
  117.4 1.2 copy-start
  118.6 1.2 copy-start.1

commit v2 on v1

--- a/solution.py
+++ b/solution.py
@@ -9,6 +9,7 @@
 CHUNK = 256
 F32 = jnp.float32
 BF16 = jnp.bfloat16
+CORE_AT = 8 * 224
 MAP_START = (3, 3 + 112, 3 + 112 + 120)
 
 
@@ -31,10 +32,19 @@
 
 
 def upper_kernel(
-    info, whole, got, near, other, pivots, inverses, out,
+    info, whole, got, near, other, pivots, all_inverses, out,
     z_one, z_two, z_top, y_one, y_two, y_top, t_one, t_two, own_one, own_two, core_one, core_two,
+    couplings, top, inverses, arrived,
 ):
-    p, s, c = info[0], info[1], info[2]
+    p, s, u = info[0], info[1], info[2]
+    c = u % 2
+    copies = [
+        pltpu.make_async_copy(all_inverses.at[8:15], inverses, arrived.at[0]),
+        pltpu.make_async_copy(pivots.at[0:7, 0:BLOCK, BLOCK : 2 * BLOCK], couplings, arrived.at[1]),
+        pltpu.make_async_copy(pivots.at[6], top, arrived.at[2]),
+    ]
+    for copy in copies:
+        copy.start()
     z_refs = (None, z_one, z_two, z_top)
     y_refs = (None, y_one, y_two, y_top)
     t_refs = (None, t_one, t_two)
@@ -73,10 +83,19 @@
     def leaf_own(front, q):
         return leaf_slots(front, stacked(front, slice(256 * q, 256 * q + 256)))
 
+    def share(other_u, front, part):
+        apart = u ^ other_u
+        start = CORE_AT + apart // 2 * 384 + front * 48 + part * 16
+        at = pl.ds(pl.multiple_of(start, 16), 16)
+        return jnp.where(apart % 2 == 0, near[at, :], other[at, :])
+
     def leaf_core(front):
-        blocks = stacked(front, slice(512, 896))
-        turned = blocks[:, BLOCK : 2 * BLOCK].astype(F32).T.astype(BF16)
-        return blocks[:, : 2 * BLOCK], jnp.concatenate([turned, blocks[:, 2 * BLOCK :]], 1)
+        blocks = [
+            jnp.concatenate([share(member, front, part) for member in range(8)], 0)
+            for part in range(3)
+        ]
+        turned = blocks[1].astype(F32).T.astype(BF16)
+        return jnp.concatenate(blocks[:2], 1), jnp.concatenate([turned, blocks[2]], 1)
 
     for level in (1, 2, 3):
         z_ref, y_ref = z_refs[level], y_refs[level]
@@ -85,6 +104,7 @@
         wanted = 4 if level < 3 else 2
         z_ref[...] = jnp.zeros_like(z_ref)
         y_ref[...] = jnp.zeros_like(y_ref)
+        panels_t = []
         for front in range(8 >> level):
             kids = (2 * front, 2 * front + 1)
             goal = (0, 1, 2 * group, 2 * group + 1)
@@ -113,7 +133,8 @@
                 if level == 1:
                     for block in range(2, 16):
                         at = slice(16 * (block - 2), 16 * (block - 1))
-                        one, two = near[kid, at, :], other[kid, at, :]
+                        start = kid * 224 + 16 * (block - 2)
+                        one, two = near[start : start + 16, :], other[start : start + 16, :]
                         panel = jnp.concatenate(
                             [jnp.where(c == 0, one, two), jnp.where(c == 0, two, one)], 1
                         )
@@ -133,16 +154,18 @@
                     lax.fori_loop(2, 2 * group, step, 0, unroll=6)
 
             if level == 3:
-                lane_part = []
                 for half in range(2):
                     at = pl.ds(pl.multiple_of(half * BLOCK + 16 * s, 16), 16)
-                    strip = pivots[6, at, :]
+                    strip = top[at, :]
                     z_ref[0, 16 * half : 16 * half + 16, :] += strip
                     strip = jnp.where(p == 0, strip[:, :BLOCK], strip[:, BLOCK:])
                     strip = jnp.where(p < 2, strip, jnp.zeros_like(strip))
                     y_ref[0, 16 * half : 16 * half + 16, :BLOCK] += strip
 
             core_rows = (2, 3, 1) if level < 3 else (1,)
+            if level == 1 and front == 0:
+                for copy in copies:
+                    copy.wait()
             if level == 1:
                 kid_own = [[leaf_own(kid, q) for q in range(2)] for kid in kids]
                 kid_core = [leaf_core(kid) for kid in kids]
@@ -157,7 +180,7 @@
                         value = own_refs[level - 1][kid, (q % 2) * BLOCK : (q % 2 + 1) * BLOCK, :]
                     own = own + masked(child, q, value.astype(F32))
                 if level == 3:
-                    strip = pivots[6, q * BLOCK : (q + 1) * BLOCK, :].astype(F32)
+                    strip = top[q * BLOCK : (q + 1) * BLOCK, :].astype(F32)
                     strip = jnp.where(p == 0, strip[:, :BLOCK], strip[:, BLOCK:])
                     strip = jnp.where(p < 2, strip, jnp.zeros_like(strip))
                     own = own + jnp.concatenate([strip, jnp.zeros_like(strip)], 1)
@@ -172,47 +195,65 @@
                         part = part[:, (r % 2) * BLOCK : (r % 2 + 1) * BLOCK].astype(F32)
                         value = value + masked(child, q, masked(child, r, part))
                     if q == 0 and r == 1:
-                        value = value + pivots[
-                            8 - (16 >> level) + front, :BLOCK, BLOCK:
-                        ].astype(F32)
+                        value = value + couplings[8 - (16 >> level) + front].astype(F32)
                     parts.append(value)
                 zt.append(jnp.concatenate(parts, 1).astype(BF16))
-            live = zt[0].shape[1] - BLOCK
-            inverse_zero = inverses[16 - (16 >> level) + front, 0]
-            inverse_one = inverses[16 - (16 >> level) + front, 1]
-            columns, scaled = panels(zt[0], zt[1], inverse_zero, inverse_one, live)
-            coupling = columns[:BLOCK, live:]
-            own_scaled = scaled[:, :256]
-            if level < 3:
-                core_cols = columns[:, 256:512]
-                later = jnp.concatenate([zt[2], zt[3]], 0)[:, :512].astype(F32)
-                later = (later - dot_tn(core_cols, scaled[:, :512])).astype(BF16)
-                own_refs[level][front] = later[:, :256]
-                core_refs[level][front] = later[:, 256:]
-            for start in range(0, width, CHUNK):
-                at = pl.ds(start, CHUNK)
-                first = z_ref[front, at, :BLOCK]
-                scaled_zero = dot(first, inverse_zero).astype(BF16)
-                second = z_ref[front, at, BLOCK : 2 * BLOCK].astype(F32)
-                second = (second - dot(scaled_zero, coupling)).astype(BF16)
-                row = y_ref[front, at, :].astype(F32)
-                row = row - dot(jnp.concatenate([first, second], 1), own_scaled)
-                if level == 3:
-                    out[:, start : start + CHUNK] = row.T.astype(BF16)
-                    continue
-                y_ref[front, at, :] = row.astype(BF16)
-                scaled_one = dot(second, inverse_one).astype(BF16)
-                rest = z_ref[front, at, 2 * BLOCK :].astype(F32)
-                rest = rest - dot(jnp.concatenate([scaled_zero, scaled_one], 1), core_cols)
-                t_refs[level][front, at, :] = rest.astype(BF16)
+            panels_t.append(zt)
+
+        fronts = range(8 >> level)
+        pieces = [(front, start) for front in fronts for start in range(0, width, CHUNK)]
+        live = panels_t[0][0].shape[1] - BLOCK
+        inverse = [
+            [inverses[8 - (16 >> level) + front, q] for q in range(2)] for front in fronts
+        ]
+
+        def rows_of(ref, front, start, q):
+            return ref[front, pl.ds(start, CHUNK), q * BLOCK : (q + 1) * BLOCK]
+
+        scaled_zero_t = [dot(inverse[f][0], panels_t[f][0]).astype(BF16) for f in fronts]
+        scaled_zero = [dot(rows_of(z_ref, f, at, 0), inverse[f][0]).astype(BF16) for f, at in pieces]
+        second_t, second = [], []
+        for f in fronts:
+            coupling = panels_t[f][0][:, live:]
+            value = panels_t[f][1].astype(F32) - dot_tn(coupling, scaled_zero_t[f])
+            second_t.append(value.astype(BF16))
+        for i, (f, at) in enumerate(pieces):
+            coupling = panels_t[f][0][:, live:]
+            value = rows_of(z_ref, f, at, 1).astype(F32) - dot(scaled_zero[i], coupling)
+            second.append(value.astype(BF16))
+        scaled_one_t = [dot(inverse[f][1], second_t[f]).astype(BF16) for f in fronts]
+        if level < 3:
+            scaled_one = [dot(second[i], inverse[f][1]).astype(BF16) for i, (f, _) in enumerate(pieces)]
+            core_cols = [
+                jnp.concatenate([panels_t[f][0][:, 256:512], second_t[f][:, 256:512]], 0)
+                for f in fronts
+            ]
+            for f in fronts:
+                later = jnp.concatenate([panels_t[f][2], panels_t[f][3]], 0)[:, :512].astype(F32)
+                scaled = jnp.concatenate([scaled_zero_t[f][:, :512], scaled_one_t[f][:, :512]], 0)
+                later = (later - dot_tn(core_cols[f], scaled)).astype(BF16)
+                own_refs[level][f] = later[:, :256]
+                core_refs[level][f] = later[:, 256:]
+        for i, (f, at) in enumerate(pieces):
+            own_scaled = jnp.concatenate([scaled_zero_t[f][:, :256], scaled_one_t[f][:, :256]], 0)
+            columns = jnp.concatenate([rows_of(z_ref, f, at, 0), second[i]], 1)
+            row = y_ref[f, pl.ds(at, CHUNK), :].astype(F32) - dot(columns, own_scaled)
+            if level == 3:
+                out[:, at : at + CHUNK] = row.T.astype(BF16)
+                continue
+            y_ref[f, pl.ds(at, CHUNK), :] = row.astype(BF16)
+            rest = z_ref[f, pl.ds(at, CHUNK), 2 * BLOCK :].astype(F32)
+            rest = rest - dot(jnp.concatenate([scaled_zero[i], scaled_one[i]], 1), core_cols[f])
+            t_refs[level][f, pl.ds(at, CHUNK), :] = rest.astype(BF16)
 
 
 def upper_levels(info, whole, got, near, other, pivots, inverses):
     vmem = pl.BlockSpec(memory_space=pltpu.VMEM)
+    anywhere = pl.BlockSpec(memory_space=pltpu.HBM)
     return pl.pallas_call(
         upper_kernel,
         out_shape=jax.ShapeDtypeStruct((256, 2048), BF16),
-        in_specs=[pl.BlockSpec(memory_space=pltpu.SMEM)] + [vmem] * 6,
+        in_specs=[pl.BlockSpec(memory_space=pltpu.SMEM)] + [vmem] * 4 + [anywhere] * 2,
         out_specs=vmem,
         scratch_shapes=[
             pltpu.VMEM(shape, BF16)
@@ -221,14 +262,16 @@
                 (4, 512, 256), (2, 1024, 256), (1, 2048, 256),
                 (4, 512, 256), (2, 1024, 256),
                 (4, 256, 256), (2, 256, 256), (4, 256, 256), (2, 256, 256),
+                (7, BLOCK, BLOCK), (256, 256), (7, 2, BLOCK, BLOCK),
             )
-        ],
-        compiler_params=pltpu.CompilerParams(vmem_limit_bytes=48 * 2**20),
+        ]
+        + [pltpu.SemaphoreType.DMA((3,))],
+        compiler_params=pltpu.CompilerParams(vmem_limit_bytes=62 * 2**20),
         name="upper_levels",
     )(info, whole, got, near, other, pivots, inverses)
 
 
-def leaf_stage(leaf, inverses, zl, xl, c, s):
+def leaf_stage(leaf, inverses, zl, xl, c, u):
     tile = leaf
     spread = jnp.where(xl == 0, tile, lax.ppermute(tile, "xl", [(0, 1)]))
     spread = jnp.where(zl == 0, spread, lax.ppermute(spread, "zl", [(0, 1)]))
@@ -255,7 +298,7 @@
     core = core - dot_tn(columns[:, 640:], scaled[:, 640:])
     core = core.astype(BF16)
     core = jnp.concatenate([core[:BLOCK, :BLOCK], core[:BLOCK, BLOCK:], core[BLOCK:, BLOCK:]], 1)
-    core = lax.dynamic_slice_in_dim(core, 16 * s, 16, 0)
+    core = lax.dynamic_slice_in_dim(core, 16 * u, 16, 0)
     tile = tile.T.astype(F32) - dot_tn(columns[:, :256], scaled[:, 256:512])
     rest = jnp.concatenate([core[:8, 256:], core[8:, 256:]], 1)
     return jnp.concatenate([tile[32:].astype(BF16), core[:, :256], rest], 0)
@@ -267,28 +310,34 @@
     u = zl * 4 + xl * 2 + c
     maps = (block_map_one, block_map_two, block_map_top)
     info = jnp.concatenate(
-        [jnp.stack([k * 8 + u, s, c]).astype(jnp.int32)] + [table.reshape(-1) for table in maps]
+        [jnp.stack([k * 8 + u, s, u]).astype(jnp.int32)] + [table.reshape(-1) for table in maps]
     )
     payload = leaf_stage(
-        leaf_fronts, lax.dynamic_index_in_dim(pivot_inverse, k, 0, keepdims=False), zl, xl, c, s
+        leaf_fronts, lax.dynamic_index_in_dim(pivot_inverse, k, 0, keepdims=False), zl, xl, c, u
     )
     whole = lax.all_gather(payload, "k")
-    rest = jnp.concatenate([whole[:, 240:, :BLOCK], whole[:, 240:, BLOCK:]], 1)
-    piece = jnp.concatenate([whole[:, 96:112], whole[:, 112:128], whole[:, 224:240], rest], 2)
-    got = lax.all_to_all(jnp.broadcast_to(piece[None], (8, 8, 16, 896)), "sub", 0, 0, tiled=True)
-
-    def spread(value, axis, position):
-        return jnp.where(position == 0, value, lax.ppermute(value, axis, [(0, 1)]))
-
-    later = whole[:, :224, BLOCK:]
-    near = jnp.concatenate(
+    piece = jnp.concatenate([whole[:, 96:112], whole[:, 112:128]], 2)
+    got = lax.all_to_all(jnp.broadcast_to(piece[None], (8, 8, 16, 512)), "sub", 0, 0, tiled=True)
+    core = jnp.concatenate(
         [
-            spread(spread(later[:4], "xl", xl), "zl", zl),
-            spread(spread(later[4:], "zl", zl), "xl", xl),
+            whole[:, 224:240, :BLOCK],
+            whole[:, 224:240, BLOCK:],
+            whole[:, 240:, :BLOCK],
+            whole[:, 240:, BLOCK:],
         ],
-        0,
-    )
-    other = lax.ppermute(near, "c", [(0, 1), (1, 0)])
+        1,
+    ).reshape(384, BLOCK)
+    columns = whole[:, :224, BLOCK:].reshape(2, 896, BLOCK)
+    down, swap = [(0, 1)], [(0, 1), (1, 0)]
+    far = lax.ppermute(jnp.concatenate([columns[0], core], 0), "xl", swap)
+    one = jnp.where(xl == 0, columns[0], far[:896])
+    two = jnp.where(zl == 0, columns[1], lax.ppermute(columns[1], "zl", down))
+    cores = jnp.concatenate([core, far[896:]], 0)
+    far = lax.ppermute(jnp.concatenate([one, cores], 0), "zl", swap)
+    one = jnp.where(zl == 0, one, far[:896])
+    two = jnp.where(xl == 0, two, lax.ppermute(two, "xl", down))
+    near = jnp.concatenate([one, two, cores, far[896:]], 0)
+    other = lax.ppermute(near, "c", swap)
     return upper_levels(info, whole, got, near, other, pivot_entries, pivot_inverse)
 
 

time: 135 us -> 130 us (0.963)
  waiting for transfers between devices: 33.8 us -> 25 us
  starting transfers between devices: 40.3 us -> 44.8 us
  Pallas kernels: 14.9 us -> 11.5 us
    ppermute x5, waiting for transfers between devices: 19.1 us -> 9.39 us  [the longest x1 8.39 us: local(): two = jnp.where(xl == 0, two, lax.ppermute(two, 'xl', down))]
    ppermute x5, starting transfers between devices: 17.5 us -> 21.7 us  [the longest x1 9.55 us: local(): other = lax.ppermute(near, 'c', swap)]
    pallas_call x1, Pallas kernels: 14.9 us -> 11.5 us  [upper_levels(): pl.pallas_call(upper_kernel, out_shape=jax.ShapeDtypeStruct((256, 2048),...]
    concatenate x1 -> x2, local copies, waits for them, and re-layouts: 0.08 us -> 1.63 us  [the longest x1 0.95 us: local(): near = jnp.concatenate([one, two, cores, far[896:]], 0)]
    unnamed x16 -> x24, local copies, waits for them, and re-layouts: 3.44 us -> 2.95 us
  transfers between devices with their start and end apart: 10 -> 10, of which waited for: 6 -> 6; matrix products, arithmetic and copies ran while one was open for 2% -> 3% of each run, Pallas kernels for 0% -> 0%
where the time goes in v2:
time: 130 us; the launch traced here: 129 us
  starting transfers between devices  44.8 us (34%)
  blocking collectives  35 us (27%)
  waiting for transfers between devices  25 us (19%)
  Pallas kernels  11.5 us (9%)
  local copies, waits for them, and re-layouts  8.08 us (6%)
  matrix products  2.66 us (2%)
  other arithmetic  1.37 us (1%)
    all_gather x1, blocking collectives, local(): whole = lax.all_gather(payload, 'k')  35 us
    pallas_call x1, Pallas kernels, upper_levels(): pl.pallas_call(upper_kernel, out_shape=jax.ShapeDtypeStruct((256, 2048),...  11.5 us
    ppermute x1, starting transfers between devices, local(): other = lax.ppermute(near, 'c', swap)  9.55 us
    ppermute x1, waiting for transfers between devices, local(): two = jnp.where(xl == 0, two, lax.ppermute(two, 'xl', down))  8.39 us
    all_to_all x1, waiting for transfers between devices, leaf_stage(): lax.all_to_all(jnp.broadcast_to(piece[None], (8,) + piece.shape), 'sub',...  7.67 us
    all_to_all x1, starting transfers between devices, local(): lax.all_to_all(jnp.broadcast_to(piece[None], (8, 8, 16, 512)), 'sub', 0,...  7 us
    all_to_all x1, starting transfers between devices, leaf_stage(): lax.all_to_all(jnp.broadcast_to(piece[None], (8,) + piece.shape), 'sub',...  6.87 us
    ppermute x1, waiting for transfers between devices, leaf_stage(): spread = jnp.where(xl == 0, tile, lax.ppermute(tile, 'xl', [(0, 1)]))  5.15 us
  transfers between devices with their start and end apart: 10, of which 6 were waited for; matrix products, arithmetic and copies ran while one was open for 3% of the time, Pallas kernels for 0%

profile of v2, /device:TPU:7, one launch (start us, length us, event | category | flops | bytes accessed | tf_op | source)
XLA Modules:
  0.0 128.8 jit_solution(887696310655582490)
XLA Ops:
  0.0 1.3 collective-permute-start
  1.3 5.2 %collective-permute-done = bf16[256,256]{1,0:T(8,128)(2,1)S(1)} collective-permute-done((bf16[256,256]{1,0:T(8,128)(2,1)}, bf16[256,256]{1,0:T(8,128)(2,1)S(1)}, u32[]{:S(2)}, u32[]{:S(2)}) %collective-permute-start) | collective-permute-done | bytes 131104 | tf_op jit(solution)/shard_map/ppermute | solution.py:276
  6.5 3.5 %collective-permute-start.1 = (bf16[256,256]{1,0:T(8,128)(2,1)S(1)}, bf16[256,256]{1,0:T(8,128)(2,1)S(1)}, u32[]{:S(2)}, u32[]{:S(2)}) collective-permute-start(bf16[256,256]{1,0:T(8,128)(2,1)S(1)} %broadcast_select_fusion.1), channel_id=1, source_target_pairs={{0,32},{1,33},{2,34},{3,35},{4,36},{5,37},{6,38},{7,39},{8,40},{9,... | collective-permute-start | bytes 393224 | tf_op jit(solution)/shard_map/ppermute | solution.py:277
  10.2 1.8 %collective-permute-done.1 = bf16[256,256]{1,0:T(8,128)(2,1)S(1)} collective-permute-done((bf16[256,256]{1,0:T(8,128)(2,1)S(1)}, bf16[256,256]{1,0:T(8,128)(2,1)S(1)}, u32[]{:S(2)}, u32[]{:S(2)}) %collective-permute-start.1) | collective-permute-done | bytes 131104 | tf_op jit(solution)/shard_map/ppermute | solution.py:277
  12.0 4.3 %collective-permute-start.2 = (bf16[256,256]{1,0:T(8,128)(2,1)S(1)}, bf16[256,256]{1,0:T(8,128)(2,1)S(1)}, u32[]{:S(2)}, u32[]{:S(2)}) collective-permute-start(bf16[256,256]{1,0:T(8,128)(2,1)S(1)} %broadcast_select_fusion.2), channel_id=1, source_target_pairs={{0,8},{8,0},{1,9},{9,1},{2,10},{10,2},{3,11},{11,3},{4,12},{12,4},... | collective-permute-start | bytes 393224 | tf_op jit(solution)/shard_map/ppermute | solution.py:278
  16.3 1.0 collective-permute-done.2
  17.8 0.8 broadcast_in_dim.4
  18.6 6.9 %all-to-all-start = ((bf16[8,32,896]{2,1,0:T(8,128)(2,1)}), bf16[8,32,896]{2,1,0:T(8,128)(2,1)S(1)}, u32[]{:S(2)}, u32[]{:S(2)}) async-start(bf16[8,32,896]{2,1,0:T(8,128)(2,1)} %broadcast_in_dim.4), calls=%async_computation | async-start | bytes 917504 | tf_op jit(solution)/shard_map/all_to_all | solution.py:292
  25.6 7.7 %all-to-all-done = bf16[8,32,896]{2,1,0:T(8,128)(2,1)S(1)} async-done(((bf16[8,32,896]{2,1,0:T(8,128)(2,1)}), bf16[8,32,896]{2,1,0:T(8,128)(2,1)S(1)}, u32[]{:S(2)}, u32[]{:S(2)}) %all-to-all-start) | async-done | bytes 458784 | tf_op jit(solution)/shard_map/all_to_all | solution.py:292
  33.3 1.0 convolution_convert_fusion.1
  34.3 0.2 subtract_convert_fusion
  34.6 1.0 convolution_convert_fusion
  35.8 0.2 fusion
  36.1 0.6 copy-done.4
  36.7 0.7 slice-done
  37.4 35.0 %all-gather = bf16[1984,256]{1,0:T(8,128)(2,1)S(1)} all-gather(bf16[248,256]{1,0:T(8,128)(2,1)S(1)} %maximum_maximum_fusion), channel_id=2, replica_groups=mesh['k'=8,'zl'=2,'xl'=2,'c'=2,'sub'=8] {'k'}, dimensions={0}, use_global_device_ids=true | all-gather | bytes 1142784 | tf_op jit(solution)/shard_map/all_gather | solution.py:318
  72.6 2.2 %collective-permute-start.3 = (bf16[1280,128]{1,0:T(8,128)(2,1)S(1)}, bf16[1280,128]{1,0:T(8,128)(2,1)S(1)}, u32[]{:S(2)}, u32[]{:S(2)}) collective-permute-start(bf16[1280,128]{1,0:T(8,128)(2,1)S(1)} %pad_maximum_fusion.1), channel_id=1, source_target_pairs={{0,16},{16,0},{1,17},{17,1},{2,18},{18,2},{3,19},{19,3},{4,20},{20... | collective-permute-start | bytes 983048 | tf_op jit(solution)/shard_map/ppermute | solution.py:332
  74.8 4.6 %collective-permute-start.5 = (bf16[896,128]{1,0:T(8,128)(2,1)S(1)}, bf16[896,128]{1,0:T(8,128)(2,1)S(1)}, u32[]{:S(2)}, u32[]{:S(2)}) collective-permute-start(bf16[896,128]{1,0:T(8,128)(2,1)S(1)} %bitcast.42), channel_id=1, source_target_pairs={{0,32},{1,33},{2,34},{3,35},{4,36},{5,37},{6,38},{7,39},{8,40},{9,... | collective-permute-start | bytes 688136 | tf_op jit(solution)/shard_map/ppermute | solution.py:334
  79.4 1.0 collective-permute-done.3
  80.5 4.1 %collective-permute-start.4 = (bf16[1664,128]{1,0:T(8,128)(2,1)S(1)}, bf16[1664,128]{1,0:T(8,128)(2,1)}, u32[]{:S(2)}, u32[]{:S(2)}) collective-permute-start(bf16[1664,128]{1,0:T(8,128)(2,1)S(1)} %pad_maximum_fusion), channel_id=1, source_target_pairs={{0,32},{32,0},{1,33},{33,1},{2,34},{34,2},{3,35},{35,3},{4,36},{36... | collective-permute-start | bytes 1277960 | tf_op jit(solution)/shard_map/ppermute | solution.py:336
  84.7 1.1 broadcast_in_dim.5
  85.8 7.0 %all-to-all-start.1 = ((bf16[8,8,16,512]{3,2,1,0:T(8,128)(2,1)}), bf16[8,8,16,512]{3,2,1,0:T(8,128)(2,1)S(1)}, u32[]{:S(2)}, u32[]{:S(2)}) async-start(bf16[8,8,16,512]{3,2,1,0:T(8,128)(2,1)} %broadcast_in_dim.5), calls=%async_computation.1 | async-start | bytes 2097152 | tf_op jit(solution)/shard_map/all_to_all | solution.py:320
  92.8 1.3 %collective-permute-start.6 = (bf16[896,128]{1,0:T(8,128)(2,1)S(1)}, bf16[896,128]{1,0:T(8,128)(2,1)S(1)}, u32[]{:S(2)}, u32[]{:S(2)}) collective-permute-start(bf16[896,128]{1,0:T(8,128)(2,1)S(1)} %broadcast_select_fusion), channel_id=1, source_target_pairs={{0,16},{1,17},{2,18},{3,19},{4,20},{5,21},{6,22},{7,23},{8,24},{9,... | collective-permute-start | bytes 688136 | tf_op jit(solution)/shard_map/ppermute | solution.py:338
  94.1 1.0 fusion.1
  95.1 8.4 %collective-permute-done.6 = bf16[896,128]{1,0:T(8,128)(2,1)S(1)} collective-permute-done((bf16[896,128]{1,0:T(8,128)(2,1)S(1)}, bf16[896,128]{1,0:T(8,128)(2,1)S(1)}, u32[]{:S(2)}, u32[]{:S(2)}) %collective-permute-start.6) | collective-permute-done | bytes 229408 | tf_op jit(solution)/shard_map/ppermute | solution.py:338
  103.7 1.0 slice_dynamic-update-slice_fusion.near
  104.6 9.5 %collective-permute-start.7 = (bf16[3328,128]{1,0:T(8,128)(2,1)S(1)}, bf16[3328,128]{1,0:T(8,128)(2,1)}, u32[]{:S(2)}, u32[]{:S(2)}) collective-permute-start(bf16[3328,128]{1,0:T(8,128)(2,1)S(1)} %slice_dynamic-update-slice_fusion.near), channel_id=1, source_target_pairs={{0,8},{8,0},{1,9},{9,1},{2,10},{10,2},{3,11},{11,3},{4,12},{12,4},... | collective-permute-start | bytes 2555912 | tf_op jit(solution)/shard_map/ppermute | solution.py:340
  114.3 0.6 copy-done.6
  115.0 0.6 copy-done.7
  115.6 0.7 concatenate.46.info
  116.3 1.0 copy-done.1
  117.3 11.5 %upper_levels.1 = bf16[256,2048]{1,0:T(8,128)(2,1)} custom-call(s32[359]{0:T(512)} %concatenate.46.info, bf16[8,248,256]{2,1,0:T(8,128)(2,1)} %bitcast.34, bf16[8,8,16,512]{3,2,1,0:T(8,128)(2,1)} %copy-done.1, bf16[3328,128]{1,0:T(8,128)(2,1)} %copy-done.2, bf16[3328,128]{1,0:T(8,128)(2,1)} %collective-permute-done.7.other, bf16[7,256,256]{2,1,0:T(8,128)(2,1)} %pivots.1, ...), custom_call_target="tpu_custom_call" | custom-call | tf_op jit(solution)/shard_map/upper_levels/pallas_call | solution.py:253
  (63 shorter events, 1.7 us)
Async XLA Ops:
  0.0 6.5 %collective-permute-start = (bf16[256,256]{1,0:T(8,128)(2,1)}, bf16[256,256]{1,0:T(8,128)(2,1)S(1)}, u32[]{:S(2)}, u32[]{:S(2)}) collective-permute-start(bf16[256,256]{1,0:T(8,128)(2,1)} %param.6), channel_id=1, source_target_pairs={{0,16},{1,17},{2,18},{3,19},{4,20},{5,21},{6,22},{7,23},{8,24},{9,... | collective-permute-start | bytes 393224 | tf_op jit(solution)/shard_map/ppermute | solution.py:276
  1.3 8.7 %copy-start.3 = (bf16[256,256]{1,0:T(8,128)(2,1)S(1)}, bf16[256,256]{1,0:T(8,128)(2,1)}, u32[]{:S(2)}) copy-start(bf16[256,256]{1,0:T(8,128)(2,1)} %param.6) | copy-start | bytes 393220
  6.5 5.5 %collective-permute-start.1 = (bf16[256,256]{1,0:T(8,128)(2,1)S(1)}, bf16[256,256]{1,0:T(8,128)(2,1)S(1)}, u32[]{:S(2)}, u32[]{:S(2)}) collective-permute-start(bf16[256,256]{1,0:T(8,128)(2,1)S(1)} %broadcast_select_fusion.1), channel_id=1, source_target_pairs={{0,32},{1,33},{2,34},{3,35},{4,36},{5,37},{6,38},{7,39},{8,40},{9,... | collective-permute-start | bytes 393224 | tf_op jit(solution)/shard_map/ppermute | solution.py:277
  12.0 5.3 %collective-permute-start.2 = (bf16[256,256]{1,0:T(8,128)(2,1)S(1)}, bf16[256,256]{1,0:T(8,128)(2,1)S(1)}, u32[]{:S(2)}, u32[]{:S(2)}) collective-permute-start(bf16[256,256]{1,0:T(8,128)(2,1)S(1)} %broadcast_select_fusion.2), channel_id=1, source_target_pairs={{0,8},{8,0},{1,9},{9,1},{2,10},{10,2},{3,11},{11,3},{4,12},{12,4},... | collective-permute-start | bytes 393224 | tf_op jit(solution)/shard_map/ppermute | solution.py:278
  18.6 14.6 %all-to-all-start = ((bf16[8,32,896]{2,1,0:T(8,128)(2,1)}), bf16[8,32,896]{2,1,0:T(8,128)(2,1)S(1)}, u32[]{:S(2)}, u32[]{:S(2)}) async-start(bf16[8,32,896]{2,1,0:T(8,128)(2,1)} %broadcast_in_dim.4), calls=%async_computation | async-start | bytes 917504 | tf_op jit(solution)/shard_map/all_to_all | solution.py:292
  36.1 0.6 copy-start.4
  36.7 0.7 slice-start
  72.4 12.2 %copy-start = (bf16[1984,256]{1,0:T(8,128)(2,1)}, bf16[1984,256]{1,0:T(8,128)(2,1)S(1)}, u32[]{:S(2)}) copy-start(bf16[1984,256]{1,0:T(8,128)(2,1)S(1)} %all-gather) | copy-start | bytes 3047428
  72.6 7.8 %collective-permute-start.3 = (bf16[1280,128]{1,0:T(8,128)(2,1)S(1)}, bf16[1280,128]{1,0:T(8,128)(2,1)S(1)}, u32[]{:S(2)}, u32[]{:S(2)}) collective-permute-start(bf16[1280,128]{1,0:T(8,128)(2,1)S(1)} %pad_maximum_fusion.1), channel_id=1, source_target_pairs={{0,16},{16,0},{1,17},{17,1},{2,18},{18,2},{3,19},{19,3},{4,20},{20... | collective-permute-start | bytes 983048 | tf_op jit(solution)/shard_map/ppermute | solution.py:332
  74.8 18.0 %collective-permute-start.5 = (bf16[896,128]{1,0:T(8,128)(2,1)S(1)}, bf16[896,128]{1,0:T(8,128)(2,1)S(1)}, u32[]{:S(2)}, u32[]{:S(2)}) collective-permute-start(bf16[896,128]{1,0:T(8,128)(2,1)S(1)} %bitcast.42), channel_id=1, source_target_pairs={{0,32},{1,33},{2,34},{3,35},{4,36},{5,37},{6,38},{7,39},{8,40},{9,... | collective-permute-start | bytes 688136 | tf_op jit(solution)/shard_map/ppermute | solution.py:334
  80.5 13.6 %collective-permute-start.4 = (bf16[1664,128]{1,0:T(8,128)(2,1)S(1)}, bf16[1664,128]{1,0:T(8,128)(2,1)}, u32[]{:S(2)}, u32[]{:S(2)}) collective-permute-start(bf16[1664,128]{1,0:T(8,128)(2,1)S(1)} %pad_maximum_fusion), channel_id=1, source_target_pairs={{0,32},{32,0},{1,33},{33,1},{2,34},{34,2},{3,35},{35,3},{4,36},{36... | collective-permute-start | bytes 1277960 | tf_op jit(solution)/shard_map/ppermute | solution.py:336
  85.8 30.6 %all-to-all-start.1 = ((bf16[8,8,16,512]{3,2,1,0:T(8,128)(2,1)}), bf16[8,8,16,512]{3,2,1,0:T(8,128)(2,1)S(1)}, u32[]{:S(2)}, u32[]{:S(2)}) async-start(bf16[8,8,16,512]{3,2,1,0:T(8,128)(2,1)} %broadcast_in_dim.5), calls=%async_computation.1 | async-start | bytes 2097152 | tf_op jit(solution)/shard_map/all_to_all | solution.py:320
  92.8 10.7 %collective-permute-start.6 = (bf16[896,128]{1,0:T(8,128)(2,1)S(1)}, bf16[896,128]{1,0:T(8,128)(2,1)S(1)}, u32[]{:S(2)}, u32[]{:S(2)}) collective-permute-start(bf16[896,128]{1,0:T(8,128)(2,1)S(1)} %broadcast_select_fusion), channel_id=1, source_target_pairs={{0,16},{1,17},{2,18},{3,19},{4,20},{5,21},{6,22},{7,23},{8,24},{9,... | collective-permute-start | bytes 688136 | tf_op jit(solution)/shard_map/ppermute | solution.py:338
  104.6 11.7 %copy-start.2 = (bf16[3328,128]{1,0:T(8,128)(2,1)}, bf16[3328,128]{1,0:T(8,128)(2,1)S(1)}, u32[]{:S(2)}) copy-start(bf16[3328,128]{1,0:T(8,128)(2,1)S(1)} %slice_dynamic-update-slice_fusion.near) | copy-start | bytes 2555908
  104.6 9.6 %copy-start.5 = (s32[4,2,14]{2,1,0:T(2,128)S(1)}, s32[4,2,14]{2,1,0:T(2,128)}, u32[]{:S(2)}) copy-start(s32[4,2,14]{2,1,0:T(2,128)} %param.9) | copy-start | bytes 1348
  104.6 11.7 %collective-permute-start.7 = (bf16[3328,128]{1,0:T(8,128)(2,1)S(1)}, bf16[3328,128]{1,0:T(8,128)(2,1)}, u32[]{:S(2)}, u32[]{:S(2)}) collective-permute-start(bf16[3328,128]{1,0:T(8,128)(2,1)S(1)} %slice_dynamic-update-slice_fusion.near), channel_id=1, source_target_pairs={{0,8},{8,0},{1,9},{9,1},{2,10},{10,2},{3,11},{11,3},{4,12},{12,4},... | collective-permute-start | bytes 2555912 | tf_op jit(solution)/shard_map/ppermute | solution.py:340
  114.2 0.7 copy-start.6
  114.9 0.7 copy-start.7
  116.3 1.0 copy-start.1

commit v3 on v2

--- a/solution.py
+++ b/solution.py
@@ -32,19 +32,32 @@
 
 
 def upper_kernel(
-    info, whole, got, near, other, pivots, all_inverses, out,
+    info, whole_hbm, got_hbm, near_hbm, other_hbm, pivots, all_inverses, out_hbm,
     z_one, z_two, z_top, y_one, y_two, y_top, t_one, t_two, own_one, own_two, core_one, core_two,
-    couplings, top, inverses, arrived,
+    couplings, top, inverses, whole, got, near, other, out, arrived, left,
 ):
     p, s, u = info[0], info[1], info[2]
     c = u % 2
     copies = [
-        pltpu.make_async_copy(all_inverses.at[8:15], inverses, arrived.at[0]),
-        pltpu.make_async_copy(pivots.at[0:7, 0:BLOCK, BLOCK : 2 * BLOCK], couplings, arrived.at[1]),
-        pltpu.make_async_copy(pivots.at[6], top, arrived.at[2]),
+        pltpu.make_async_copy(source, target, arrived.at[i])
+        for i, (source, target) in enumerate(
+            (
+                (near_hbm, near),
+                (other_hbm, other),
+                (whole_hbm, whole),
+                (got_hbm, got),
+                (all_inverses.at[8:15], inverses),
+                (pivots.at[0:7, 0:BLOCK, BLOCK : 2 * BLOCK], couplings),
+                (pivots.at[6], top),
+            )
+        )
     ]
     for copy in copies:
         copy.start()
+    for ref in (z_one, y_one, z_two, y_two, z_top, y_top):
+        ref[...] = jnp.zeros_like(ref)
+    for copy in copies[:3]:
+        copy.wait()
     z_refs = (None, z_one, z_two, z_top)
     y_refs = (None, y_one, y_two, y_top)
     t_refs = (None, t_one, t_two)
@@ -102,8 +115,6 @@
         group = 4 << level
         width = 256 << level
         wanted = 4 if level < 3 else 2
-        z_ref[...] = jnp.zeros_like(z_ref)
-        y_ref[...] = jnp.zeros_like(y_ref)
         panels_t = []
         for front in range(8 >> level):
             kids = (2 * front, 2 * front + 1)
@@ -164,7 +175,7 @@
 
             core_rows = (2, 3, 1) if level < 3 else (1,)
             if level == 1 and front == 0:
-                for copy in copies:
+                for copy in copies[3:]:
                     copy.wait()
             if level == 1:
                 kid_own = [[leaf_own(kid, q) for q in range(2)] for kid in kids]
@@ -239,22 +250,28 @@
             columns = jnp.concatenate([rows_of(z_ref, f, at, 0), second[i]], 1)
             row = y_ref[f, pl.ds(at, CHUNK), :].astype(F32) - dot(columns, own_scaled)
             if level == 3:
-                out[:, at : at + CHUNK] = row.T.astype(BF16)
+                out[i] = row.T.astype(BF16)
+                copy = pltpu.make_async_copy(
+                    out.at[i], out_hbm.at[:, pl.ds(at, CHUNK)], left.at[i]
+                )
+                copy.start()
+                copies.append(copy)
                 continue
             y_ref[f, pl.ds(at, CHUNK), :] = row.astype(BF16)
             rest = z_ref[f, pl.ds(at, CHUNK), 2 * BLOCK :].astype(F32)
             rest = rest - dot(jnp.concatenate([scaled_zero[i], scaled_one[i]], 1), core_cols[f])
             t_refs[level][f, pl.ds(at, CHUNK), :] = rest.astype(BF16)
+    for copy in copies[7:]:
+        copy.wait()
 
 
 def upper_levels(info, whole, got, near, other, pivots, inverses):
-    vmem = pl.BlockSpec(memory_space=pltpu.VMEM)
     anywhere = pl.BlockSpec(memory_space=pltpu.HBM)
     return pl.pallas_call(
         upper_kernel,
         out_shape=jax.ShapeDtypeStruct((256, 2048), BF16),
-        in_specs=[pl.BlockSpec(memory_space=pltpu.SMEM)] + [vmem] * 4 + [anywhere] * 2,
-        out_specs=vmem,
+        in_specs=[pl.BlockSpec(memory_space=pltpu.SMEM)] + [pl.BlockSpec(memory_space=pl.ANY)] * 4 + [anywhere] * 2,
+        out_specs=anywhere,
         scratch_shapes=[
             pltpu.VMEM(shape, BF16)
             for shape in (
@@ -263,9 +280,10 @@
                 (4, 512, 256), (2, 1024, 256),
                 (4, 256, 256), (2, 256, 256), (4, 256, 256), (2, 256, 256),
                 (7, BLOCK, BLOCK), (256, 256), (7, 2, BLOCK, BLOCK),
+                whole.shape, got.shape, near.shape, other.shape, (8, 256, CHUNK),
             )
         ]
-        + [pltpu.SemaphoreType.DMA((3,))],
+        + [pltpu.SemaphoreType.DMA((7,)), pltpu.SemaphoreType.DMA((8,))],
         compiler_params=pltpu.CompilerParams(vmem_limit_bytes=62 * 2**20),
         name="upper_levels",
     )(info, whole, got, near, other, pivots, inverses)
@@ -297,11 +315,12 @@
     core = got[:, :, 640:].reshape(256, 256).astype(F32)
     core = core - dot_tn(columns[:, 640:], scaled[:, 640:])
     core = core.astype(BF16)
-    core = jnp.concatenate([core[:BLOCK, :BLOCK], core[:BLOCK, BLOCK:], core[BLOCK:, BLOCK:]], 1)
-    core = lax.dynamic_slice_in_dim(core, 16 * u, 16, 0)
+    upper = lax.dynamic_slice_in_dim(core[:BLOCK], 16 * u, 16, 0)
+    lower = lax.dynamic_slice_in_dim(core[BLOCK:, BLOCK:], 16 * u, 16, 0)
     tile = tile.T.astype(F32) - dot_tn(columns[:, :256], scaled[:, 256:512])
-    rest = jnp.concatenate([core[:8, 256:], core[8:, 256:]], 1)
-    return jnp.concatenate([tile[32:].astype(BF16), core[:, :256], rest], 0)
+    return jnp.concatenate(
+        [tile[32:].astype(BF16), upper, jnp.concatenate([lower[:8], lower[8:]], 1)], 0
+    )
 
 
 def local(leaf_fronts, pivot_entries, pivot_inverse, block_map_one, block_map_two, block_map_top):

time: 130 us -> 128 us (0.985)
    unnamed x24 -> x22, local copies, waits for them, and re-layouts: 2.95 us -> 2.38 us
where the time goes in v3:
time: 128 us; the launch traced here: 127 us
  starting transfers between devices  44.8 us (35%)
  blocking collectives  35 us (27%)
  waiting for transfers between devices  25 us (20%)
  Pallas kernels  10.8 us (8%)
  local copies, waits for them, and re-layouts  6.85 us (5%)
  matrix products  2.66 us (2%)
  other arithmetic  1.36 us (1%)
    all_gather x1, blocking collectives, local(): whole = lax.all_gather(payload, 'k')  35 us
    pallas_call x1, Pallas kernels, upper_levels(): pl.pallas_call(upper_kernel, out_shape=jax.ShapeDtypeStruct((256, 2048),...  10.8 us
    ppermute x1, starting transfers between devices, local(): other = lax.ppermute(near, 'c', swap)  9.55 us
    ppermute x1, waiting for transfers between devices, local(): two = jnp.where(xl == 0, two, lax.ppermute(two, 'xl', down))  8.39 us
    all_to_all x1, waiting for transfers between devices, leaf_stage(): lax.all_to_all(jnp.broadcast_to(piece[None], (8,) + piece.shape), 'sub',...  7.67 us
    all_to_all x1, starting transfers between devices, local(): lax.all_to_all(jnp.broadcast_to(piece[None], (8, 8, 16, 512)), 'sub', 0,...  7 us
    all_to_all x1, starting transfers between devices, leaf_stage(): lax.all_to_all(jnp.broadcast_to(piece[None], (8,) + piece.shape), 'sub',...  6.87 us
    ppermute x1, waiting for transfers between devices, leaf_stage(): spread = jnp.where(xl == 0, tile, lax.ppermute(tile, 'xl', [(0, 1)]))  5.15 us
  transfers between devices with their start and end apart: 10, of which 6 were waited for; matrix products, arithmetic and copies ran while one was open for 3% of the time, Pallas kernels for 0%

profile of v3, /device:TPU:7, one launch (start us, length us, event | category | flops | bytes accessed | tf_op | source)
XLA Modules:
  0.0 126.9 jit_solution(12532742497103325490)
XLA Ops:
  0.0 1.3 %collective-permute-start = (bf16[256,256]{1,0:T(8,128)(2,1)}, bf16[256,256]{1,0:T(8,128)(2,1)S(1)}, u32[]{:S(2)}, u32[]{:S(2)}) collective-permute-start(bf16[256,256]{1,0:T(8,128)(2,1)} %param.6), channel_id=1, source_target_pairs={{0,16},{1,17},{2,18},{3,19},{4,20},{5,21},{6,22},{7,23},{8,24},{9,... | collective-permute-start | bytes 393224 | tf_op jit(solution)/shard_map/ppermute | solution.py:294
  1.3 5.2 %collective-permute-done = bf16[256,256]{1,0:T(8,128)(2,1)S(1)} collective-permute-done((bf16[256,256]{1,0:T(8,128)(2,1)}, bf16[256,256]{1,0:T(8,128)(2,1)S(1)}, u32[]{:S(2)}, u32[]{:S(2)}) %collective-permute-start) | collective-permute-done | bytes 131104 | tf_op jit(solution)/shard_map/ppermute | solution.py:294
  6.5 3.5 %collective-permute-start.1 = (bf16[256,256]{1,0:T(8,128)(2,1)S(1)}, bf16[256,256]{1,0:T(8,128)(2,1)S(1)}, u32[]{:S(2)}, u32[]{:S(2)}) collective-permute-start(bf16[256,256]{1,0:T(8,128)(2,1)S(1)} %broadcast_select_fusion.1), channel_id=1, source_target_pairs={{0,32},{1,33},{2,34},{3,35},{4,36},{5,37},{6,38},{7,39},{8,40},{9,... | collective-permute-start | bytes 393224 | tf_op jit(solution)/shard_map/ppermute | solution.py:295
  10.0 0.1 copy.12
  10.2 1.8 %collective-permute-done.1 = bf16[256,256]{1,0:T(8,128)(2,1)S(1)} collective-permute-done((bf16[256,256]{1,0:T(8,128)(2,1)S(1)}, bf16[256,256]{1,0:T(8,128)(2,1)S(1)}, u32[]{:S(2)}, u32[]{:S(2)}) %collective-permute-start.1) | collective-permute-done | bytes 131104 | tf_op jit(solution)/shard_map/ppermute | solution.py:295
  12.0 4.3 %collective-permute-start.2 = (bf16[256,256]{1,0:T(8,128)(2,1)S(1)}, bf16[256,256]{1,0:T(8,128)(2,1)S(1)}, u32[]{:S(2)}, u32[]{:S(2)}) collective-permute-start(bf16[256,256]{1,0:T(8,128)(2,1)S(1)} %broadcast_select_fusion.2), channel_id=1, source_target_pairs={{0,8},{8,0},{1,9},{9,1},{2,10},{10,2},{3,11},{11,3},{4,12},{12,4},... | collective-permute-start | bytes 393224 | tf_op jit(solution)/shard_map/ppermute | solution.py:296
  16.3 1.0 collective-permute-done.2
  17.8 0.8 broadcast_in_dim.4
  18.6 6.9 %all-to-all-start = ((bf16[8,32,896]{2,1,0:T(8,128)(2,1)}), bf16[8,32,896]{2,1,0:T(8,128)(2,1)S(1)}, u32[]{:S(2)}, u32[]{:S(2)}) async-start(bf16[8,32,896]{2,1,0:T(8,128)(2,1)} %broadcast_in_dim.4), calls=%async_computation | async-start | bytes 917504 | tf_op jit(solution)/shard_map/all_to_all | solution.py:310
  25.6 7.7 %all-to-all-done = bf16[8,32,896]{2,1,0:T(8,128)(2,1)S(1)} async-done(((bf16[8,32,896]{2,1,0:T(8,128)(2,1)}), bf16[8,32,896]{2,1,0:T(8,128)(2,1)S(1)}, u32[]{:S(2)}, u32[]{:S(2)}) %all-to-all-start) | async-done | bytes 458784 | tf_op jit(solution)/shard_map/all_to_all | solution.py:310
  33.3 1.0 convolution_convert_fusion.1
  34.3 0.2 subtract_convert_fusion
  34.6 1.0 convolution_convert_fusion
  35.5 0.2 fusion.8
  35.8 0.2 fusion
  36.1 35.0 %all-gather = bf16[1984,256]{1,0:T(8,128)(2,1)S(1)} all-gather(bf16[248,256]{1,0:T(8,128)(2,1)S(1)} %maximum_maximum_fusion), channel_id=2, replica_groups=mesh['k'=8,'zl'=2,'xl'=2,'c'=2,'sub'=8] {'k'}, dimensions={0}, use_global_device_ids=true | all-gather | bytes 1142784 | tf_op jit(solution)/shard_map/all_gather | solution.py:337
  71.4 2.2 %collective-permute-start.3 = (bf16[1280,128]{1,0:T(8,128)(2,1)S(1)}, bf16[1280,128]{1,0:T(8,128)(2,1)S(1)}, u32[]{:S(2)}, u32[]{:S(2)}) collective-permute-start(bf16[1280,128]{1,0:T(8,128)(2,1)S(1)} %pad_maximum_fusion.1), channel_id=1, source_target_pairs={{0,16},{16,0},{1,17},{17,1},{2,18},{18,2},{3,19},{19,3},{4,20},{20... | collective-permute-start | bytes 983048 | tf_op jit(solution)/shard_map/ppermute | solution.py:351
  73.5 4.6 %collective-permute-start.5 = (bf16[896,128]{1,0:T(8,128)(2,1)S(1)}, bf16[896,128]{1,0:T(8,128)(2,1)S(1)}, u32[]{:S(2)}, u32[]{:S(2)}) collective-permute-start(bf16[896,128]{1,0:T(8,128)(2,1)S(1)} %bitcast.42), channel_id=1, source_target_pairs={{0,32},{1,33},{2,34},{3,35},{4,36},{5,37},{6,38},{7,39},{8,40},{9,... | collective-permute-start | bytes 688136 | tf_op jit(solution)/shard_map/ppermute | solution.py:353
  78.2 1.0 collective-permute-done.3
  79.3 4.1 %collective-permute-start.4 = (bf16[1664,128]{1,0:T(8,128)(2,1)S(1)}, bf16[1664,128]{1,0:T(8,128)(2,1)}, u32[]{:S(2)}, u32[]{:S(2)}) collective-permute-start(bf16[1664,128]{1,0:T(8,128)(2,1)S(1)} %pad_maximum_fusion), channel_id=1, source_target_pairs={{0,32},{32,0},{1,33},{33,1},{2,34},{34,2},{3,35},{35,3},{4,36},{36... | collective-permute-start | bytes 1277960 | tf_op jit(solution)/shard_map/ppermute | solution.py:355
  83.4 1.1 broadcast_in_dim.5
  84.5 7.0 %all-to-all-start.1 = ((bf16[8,8,16,512]{3,2,1,0:T(8,128)(2,1)}), bf16[8,8,16,512]{3,2,1,0:T(8,128)(2,1)S(1)}, u32[]{:S(2)}, u32[]{:S(2)}) async-start(bf16[8,8,16,512]{3,2,1,0:T(8,128)(2,1)} %broadcast_in_dim.5), calls=%async_computation.1 | async-start | bytes 2097152 | tf_op jit(solution)/shard_map/all_to_all | solution.py:339
  91.6 1.3 %collective-permute-start.6 = (bf16[896,128]{1,0:T(8,128)(2,1)S(1)}, bf16[896,128]{1,0:T(8,128)(2,1)S(1)}, u32[]{:S(2)}, u32[]{:S(2)}) collective-permute-start(bf16[896,128]{1,0:T(8,128)(2,1)S(1)} %broadcast_select_fusion), channel_id=1, source_target_pairs={{0,16},{1,17},{2,18},{3,19},{4,20},{5,21},{6,22},{7,23},{8,24},{9,... | collective-permute-start | bytes 688136 | tf_op jit(solution)/shard_map/ppermute | solution.py:357
  92.9 1.0 fusion.1
  93.9 8.4 %collective-permute-done.6 = bf16[896,128]{1,0:T(8,128)(2,1)S(1)} collective-permute-done((bf16[896,128]{1,0:T(8,128)(2,1)S(1)}, bf16[896,128]{1,0:T(8,128)(2,1)S(1)}, u32[]{:S(2)}, u32[]{:S(2)}) %collective-permute-start.6) | collective-permute-done | bytes 229408 | tf_op jit(solution)/shard_map/ppermute | solution.py:357
  102.4 1.0 slice_dynamic-update-slice_fusion.near_hbm
  103.4 9.5 %collective-permute-start.7 = (bf16[3328,128]{1,0:T(8,128)(2,1)S(1)}, bf16[3328,128]{1,0:T(8,128)(2,1)}, u32[]{:S(2)}, u32[]{:S(2)}) collective-permute-start(bf16[3328,128]{1,0:T(8,128)(2,1)S(1)} %slice_dynamic-update-slice_fusion.near_hbm), channel_id=1, source_target_pairs={{0,8},{8,0},{1,9},{9,1},{2,10},{10,2},{3,11},{11,3},{4,12},{12,4},... | collective-permute-start | bytes 2555912 | tf_op jit(solution)/shard_map/ppermute | solution.py:359
  113.1 0.6 copy-done.5
  113.7 0.6 copy-done.6
  114.4 0.7 concatenate.42.info
  115.1 1.0 copy-done.1
  116.1 10.8 %upper_levels.1 = bf16[256,2048]{1,0:T(8,128)(2,1)} custom-call(s32[359]{0:T(512)} %concatenate.42.info, bf16[8,248,256]{2,1,0:T(8,128)(2,1)} %bitcast.34, bf16[8,8,16,512]{3,2,1,0:T(8,128)(2,1)} %copy-done.1, bf16[3328,128]{1,0:T(8,128)(2,1)} %copy-done.2, bf16[3328,128]{1,0:T(8,128)(2,1)} %collective-permute-done.7.other_hbm, bf16[7,256,256]{2,1,0:T(8,128)(2,1)} %pivots.1, ...), custom_call_target="tpu_custom_call" | custom-call | tf_op jit(solution)/shard_map/upper_levels/pallas_call | solution.py:270
  (59 shorter events, 1.4 us)
Async XLA Ops:
  0.0 6.5 %collective-permute-start = (bf16[256,256]{1,0:T(8,128)(2,1)}, bf16[256,256]{1,0:T(8,128)(2,1)S(1)}, u32[]{:S(2)}, u32[]{:S(2)}) collective-permute-start(bf16[256,256]{1,0:T(8,128)(2,1)} %param.6), channel_id=1, source_target_pairs={{0,16},{1,17},{2,18},{3,19},{4,20},{5,21},{6,22},{7,23},{8,24},{9,... | collective-permute-start | bytes 393224 | tf_op jit(solution)/shard_map/ppermute | solution.py:294
  1.3 8.7 %copy-start.3 = (bf16[256,256]{1,0:T(8,128)(2,1)S(1)}, bf16[256,256]{1,0:T(8,128)(2,1)}, u32[]{:S(2)}) copy-start(bf16[256,256]{1,0:T(8,128)(2,1)} %param.6) | copy-start | bytes 393220
  6.5 5.5 %collective-permute-start.1 = (bf16[256,256]{1,0:T(8,128)(2,1)S(1)}, bf16[256,256]{1,0:T(8,128)(2,1)S(1)}, u32[]{:S(2)}, u32[]{:S(2)}) collective-permute-start(bf16[256,256]{1,0:T(8,128)(2,1)S(1)} %broadcast_select_fusion.1), channel_id=1, source_target_pairs={{0,32},{1,33},{2,34},{3,35},{4,36},{5,37},{6,38},{7,39},{8,40},{9,... | collective-permute-start | bytes 393224 | tf_op jit(solution)/shard_map/ppermute | solution.py:295
  12.0 5.3 %collective-permute-start.2 = (bf16[256,256]{1,0:T(8,128)(2,1)S(1)}, bf16[256,256]{1,0:T(8,128)(2,1)S(1)}, u32[]{:S(2)}, u32[]{:S(2)}) collective-permute-start(bf16[256,256]{1,0:T(8,128)(2,1)S(1)} %broadcast_select_fusion.2), channel_id=1, source_target_pairs={{0,8},{8,0},{1,9},{9,1},{2,10},{10,2},{3,11},{11,3},{4,12},{12,4},... | collective-permute-start | bytes 393224 | tf_op jit(solution)/shard_map/ppermute | solution.py:296
  18.6 14.6 %all-to-all-start = ((bf16[8,32,896]{2,1,0:T(8,128)(2,1)}), bf16[8,32,896]{2,1,0:T(8,128)(2,1)S(1)}, u32[]{:S(2)}, u32[]{:S(2)}) async-start(bf16[8,32,896]{2,1,0:T(8,128)(2,1)} %broadcast_in_dim.4), calls=%async_computation | async-start | bytes 917504 | tf_op jit(solution)/shard_map/all_to_all | solution.py:310
  71.2 12.2 %copy-start = (bf16[1984,256]{1,0:T(8,128)(2,1)}, bf16[1984,256]{1,0:T(8,128)(2,1)S(1)}, u32[]{:S(2)}) copy-start(bf16[1984,256]{1,0:T(8,128)(2,1)S(1)} %all-gather) | copy-start | bytes 3047428
  71.4 7.8 %collective-permute-start.3 = (bf16[1280,128]{1,0:T(8,128)(2,1)S(1)}, bf16[1280,128]{1,0:T(8,128)(2,1)S(1)}, u32[]{:S(2)}, u32[]{:S(2)}) collective-permute-start(bf16[1280,128]{1,0:T(8,128)(2,1)S(1)} %pad_maximum_fusion.1), channel_id=1, source_target_pairs={{0,16},{16,0},{1,17},{17,1},{2,18},{18,2},{3,19},{19,3},{4,20},{20... | collective-permute-start | bytes 983048 | tf_op jit(solution)/shard_map/ppermute | solution.py:351
  73.5 18.0 %collective-permute-start.5 = (bf16[896,128]{1,0:T(8,128)(2,1)S(1)}, bf16[896,128]{1,0:T(8,128)(2,1)S(1)}, u32[]{:S(2)}, u32[]{:S(2)}) collective-permute-start(bf16[896,128]{1,0:T(8,128)(2,1)S(1)} %bitcast.42), channel_id=1, source_target_pairs={{0,32},{1,33},{2,34},{3,35},{4,36},{5,37},{6,38},{7,39},{8,40},{9,... | collective-permute-start | bytes 688136 | tf_op jit(solution)/shard_map/ppermute | solution.py:353
  79.3 13.6 %collective-permute-start.4 = (bf16[1664,128]{1,0:T(8,128)(2,1)S(1)}, bf16[1664,128]{1,0:T(8,128)(2,1)}, u32[]{:S(2)}, u32[]{:S(2)}) collective-permute-start(bf16[1664,128]{1,0:T(8,128)(2,1)S(1)} %pad_maximum_fusion), channel_id=1, source_target_pairs={{0,32},{32,0},{1,33},{33,1},{2,34},{34,2},{3,35},{35,3},{4,36},{36... | collective-permute-start | bytes 1277960 | tf_op jit(solution)/shard_map/ppermute | solution.py:355
  84.5 30.6 %all-to-all-start.1 = ((bf16[8,8,16,512]{3,2,1,0:T(8,128)(2,1)}), bf16[8,8,16,512]{3,2,1,0:T(8,128)(2,1)S(1)}, u32[]{:S(2)}, u32[]{:S(2)}) async-start(bf16[8,8,16,512]{3,2,1,0:T(8,128)(2,1)} %broadcast_in_dim.5), calls=%async_computation.1 | async-start | bytes 2097152 | tf_op jit(solution)/shard_map/all_to_all | solution.py:339
  91.6 10.7 %collective-permute-start.6 = (bf16[896,128]{1,0:T(8,128)(2,1)S(1)}, bf16[896,128]{1,0:T(8,128)(2,1)S(1)}, u32[]{:S(2)}, u32[]{:S(2)}) collective-permute-start(bf16[896,128]{1,0:T(8,128)(2,1)S(1)} %broadcast_select_fusion), channel_id=1, source_target_pairs={{0,16},{1,17},{2,18},{3,19},{4,20},{5,21},{6,22},{7,23},{8,24},{9,... | collective-permute-start | bytes 688136 | tf_op jit(solution)/shard_map/ppermute | solution.py:357
  103.4 11.7 %copy-start.2 = (bf16[3328,128]{1,0:T(8,128)(2,1)}, bf16[3328,128]{1,0:T(8,128)(2,1)S(1)}, u32[]{:S(2)}) copy-start(bf16[3328,128]{1,0:T(8,128)(2,1)S(1)} %slice_dynamic-update-slice_fusion.near_hbm) | copy-start | bytes 2555908
  103.4 9.6 %copy-start.4 = (s32[4,2,14]{2,1,0:T(2,128)S(1)}, s32[4,2,14]{2,1,0:T(2,128)}, u32[]{:S(2)}) copy-start(s32[4,2,14]{2,1,0:T(2,128)} %param.9) | copy-start | bytes 1348
  103.4 11.7 %collective-permute-start.7 = (bf16[3328,128]{1,0:T(8,128)(2,1)S(1)}, bf16[3328,128]{1,0:T(8,128)(2,1)}, u32[]{:S(2)}, u32[]{:S(2)}) collective-permute-start(bf16[3328,128]{1,0:T(8,128)(2,1)S(1)} %slice_dynamic-update-slice_fusion.near_hbm), channel_id=1, source_target_pairs={{0,8},{8,0},{1,9},{9,1},{2,10},{10,2},{3,11},{11,3},{4,12},{12,4},... | collective-permute-start | bytes 2555912 | tf_op jit(solution)/shard_map/ppermute | solution.py:359
  113.0 0.7 copy-start.5
  113.6 0.7 copy-start.6
  115.1 1.0 copy-start.1

commit v4 on v3

--- a/solution.py
+++ b/solution.py
@@ -10,6 +10,7 @@
 F32 = jnp.float32
 BF16 = jnp.bfloat16
 CORE_AT = 8 * 224
+SPLIT = 6 * 224
 MAP_START = (3, 3 + 112, 3 + 112 + 120)
 
 
@@ -346,16 +347,17 @@
         ],
         1,
     ).reshape(384, BLOCK)
-    columns = whole[:, :224, BLOCK:].reshape(2, 896, BLOCK)
+    columns = whole[:, :224, BLOCK:].reshape(CORE_AT, BLOCK)
+    first, second = columns[:SPLIT], columns[SPLIT:]
     down, swap = [(0, 1)], [(0, 1), (1, 0)]
-    far = lax.ppermute(jnp.concatenate([columns[0], core], 0), "xl", swap)
-    one = jnp.where(xl == 0, columns[0], far[:896])
-    two = jnp.where(zl == 0, columns[1], lax.ppermute(columns[1], "zl", down))
-    cores = jnp.concatenate([core, far[896:]], 0)
+    far = lax.ppermute(jnp.concatenate([first, core], 0), "xl", swap)
+    one = jnp.where(xl == 0, first, far[:SPLIT])
+    two = jnp.where(zl == 0, second, lax.ppermute(second, "zl", down))
+    cores = jnp.concatenate([core, far[SPLIT:]], 0)
     far = lax.ppermute(jnp.concatenate([one, cores], 0), "zl", swap)
-    one = jnp.where(zl == 0, one, far[:896])
+    one = jnp.where(zl == 0, one, far[:SPLIT])
     two = jnp.where(xl == 0, two, lax.ppermute(two, "xl", down))
-    near = jnp.concatenate([one, two, cores, far[896:]], 0)
+    near = jnp.concatenate([one, two, cores, far[SPLIT:]], 0)
     other = lax.ppermute(near, "c", swap)
     return upper_levels(info, whole, got, near, other, pivot_entries, pivot_inverse)
 

time: 128 us -> 125 us (0.977)
    ppermute x1, waiting for transfers between devices: 8.39 us -> 5.7 us  [local(): two = jnp.where(xl == 0, two, lax.ppermute(two, 'xl', down))]
    ppermute x2, waiting for transfers between devices: 0.99 us -> 2.65 us  [the longest x1 2.65 us: local(): far = lax.ppermute(jnp.concatenate([first, core], 0), 'xl', swap)]
  transfers between devices with their start and end apart: 10 -> 10, of which waited for: 6 -> 7; matrix products, arithmetic and copies ran while one was open for 3% -> 4% of each run, Pallas kernels for 0% -> 0%
where the time goes in v4:
time: 125 us
  starting transfers between devices  44.7 us (36%)
  blocking collectives  34.9 us (28%)
  waiting for transfers between devices  24.2 us (19%)
  Pallas kernels  10.8 us (9%)
  local copies, waits for them, and re-layouts  5.58 us (4%)
  matrix products  2.66 us (2%)
  other arithmetic  1.41 us (1%)
    all_gather x1, blocking collectives, local(): whole = lax.all_gather(payload, 'k')  34.9 us
    pallas_call x1, Pallas kernels, upper_levels(): pl.pallas_call(upper_kernel, out_shape=jax.ShapeDtypeStruct((256, 2048),...  10.8 us
    ppermute x1, starting transfers between devices, local(): other = lax.ppermute(near, 'c', swap)  9.68 us
    all_to_all x1, waiting for transfers between devices, leaf_stage(): lax.all_to_all(jnp.broadcast_to(piece[None], (8,) + piece.shape), 'sub',...  7.67 us
    all_to_all x1, starting transfers between devices, leaf_stage(): lax.all_to_all(jnp.broadcast_to(piece[None], (8,) + piece.shape), 'sub',...  6.87 us
    all_to_all x1, starting transfers between devices, local(): lax.all_to_all(jnp.broadcast_to(piece[None], (8, 8, 16, 512)), 'sub', 0,...  6.82 us
    ppermute x1, waiting for transfers between devices, local(): two = jnp.where(xl == 0, two, lax.ppermute(two, 'xl', down))  5.7 us
    ppermute x1, waiting for transfers between devices, leaf_stage(): spread = jnp.where(xl == 0, tile, lax.ppermute(tile, 'xl', [(0, 1)]))  5.16 us
  transfers between devices with their start and end apart: 10, of which 7 were waited for; matrix products, arithmetic and copies ran while one was open for 4% of the time, Pallas kernels for 0%

profile of v4, /device:TPU:7, one launch (start us, length us, event | category | flops | bytes accessed | tf_op | source)
XLA Modules:
  0.0 124.7 jit_solution(1153911430379342150)
XLA Ops:
  0.0 1.3 %collective-permute-start = (bf16[256,256]{1,0:T(8,128)(2,1)}, bf16[256,256]{1,0:T(8,128)(2,1)S(1)}, u32[]{:S(2)}, u32[]{:S(2)}) collective-permute-start(bf16[256,256]{1,0:T(8,128)(2,1)} %param.6), channel_id=1, source_target_pairs={{0,16},{1,17},{2,18},{3,19},{4,20},{5,21},{6,22},{7,23},{8,24},{9,... | collective-permute-start | bytes 393224 | tf_op jit(solution)/shard_map/ppermute | solution.py:295
  1.3 5.2 %collective-permute-done = bf16[256,256]{1,0:T(8,128)(2,1)S(1)} collective-permute-done((bf16[256,256]{1,0:T(8,128)(2,1)}, bf16[256,256]{1,0:T(8,128)(2,1)S(1)}, u32[]{:S(2)}, u32[]{:S(2)}) %collective-permute-start) | collective-permute-done | bytes 131104 | tf_op jit(solution)/shard_map/ppermute | solution.py:295
  6.5 3.5 %collective-permute-start.1 = (bf16[256,256]{1,0:T(8,128)(2,1)S(1)}, bf16[256,256]{1,0:T(8,128)(2,1)S(1)}, u32[]{:S(2)}, u32[]{:S(2)}) collective-permute-start(bf16[256,256]{1,0:T(8,128)(2,1)S(1)} %broadcast_select_fusion), channel_id=1, source_target_pairs={{0,32},{1,33},{2,34},{3,35},{4,36},{5,37},{6,38},{7,39},{8,40},{9,... | collective-permute-start | bytes 393224 | tf_op jit(solution)/shard_map/ppermute | solution.py:296
  10.0 1.0 copy.12
  11.1 0.9 collective-permute-done.1
  12.0 4.3 %collective-permute-start.2 = (bf16[256,256]{1,0:T(8,128)(2,1)S(1)}, bf16[256,256]{1,0:T(8,128)(2,1)S(1)}, u32[]{:S(2)}, u32[]{:S(2)}) collective-permute-start(bf16[256,256]{1,0:T(8,128)(2,1)S(1)} %broadcast_select_fusion.1), channel_id=1, source_target_pairs={{0,8},{8,0},{1,9},{9,1},{2,10},{10,2},{3,11},{11,3},{4,12},{12,4},... | collective-permute-start | bytes 393224 | tf_op jit(solution)/shard_map/ppermute | solution.py:297
  16.3 1.0 collective-permute-done.2
  17.5 0.1 copy.16
  17.6 0.1 copy.17
  17.8 0.8 broadcast_in_dim.4
  18.6 6.9 %all-to-all-start = ((bf16[8,32,896]{2,1,0:T(8,128)(2,1)}), bf16[8,32,896]{2,1,0:T(8,128)(2,1)S(1)}, u32[]{:S(2)}, u32[]{:S(2)}) async-start(bf16[8,32,896]{2,1,0:T(8,128)(2,1)} %broadcast_in_dim.4), calls=%async_computation | async-start | bytes 917504 | tf_op jit(solution)/shard_map/all_to_all | solution.py:311
  25.6 7.7 %all-to-all-done = bf16[8,32,896]{2,1,0:T(8,128)(2,1)S(1)} async-done(((bf16[8,32,896]{2,1,0:T(8,128)(2,1)}), bf16[8,32,896]{2,1,0:T(8,128)(2,1)S(1)}, u32[]{:S(2)}, u32[]{:S(2)}) %all-to-all-start) | async-done | bytes 458784 | tf_op jit(solution)/shard_map/all_to_all | solution.py:311
  33.3 1.0 convolution_convert_fusion.1
  34.3 0.2 subtract_convert_fusion
  34.6 1.0 convolution_convert_fusion
  35.5 0.2 fusion.8
  35.8 0.2 fusion
  36.1 34.9 %all-gather = bf16[1984,256]{1,0:T(8,128)(2,1)S(1)} all-gather(bf16[248,256]{1,0:T(8,128)(2,1)S(1)} %maximum_maximum_fusion), channel_id=2, replica_groups=mesh['k'=8,'zl'=2,'xl'=2,'c'=2,'sub'=8] {'k'}, dimensions={0}, use_global_device_ids=true | all-gather | bytes 1142784 | tf_op jit(solution)/shard_map/all_gather | solution.py:338
  71.2 2.3 %collective-permute-start.3 = (bf16[1728,128]{1,0:T(8,128)(2,1)S(1)}, bf16[1728,128]{1,0:T(8,128)(2,1)S(1)}, u32[]{:S(2)}, u32[]{:S(2)}) collective-permute-start(bf16[1728,128]{1,0:T(8,128)(2,1)S(1)} %pad_maximum_fusion.1), channel_id=1, source_target_pairs={{0,16},{16,0},{1,17},{17,1},{2,18},{18,2},{3,19},{19,3},{4,20},{20... | collective-permute-start | bytes 1327112 | tf_op jit(solution)/shard_map/ppermute | solution.py:353
  73.6 4.0 %collective-permute-start.5 = (bf16[448,128]{1,0:T(8,128)(2,1)S(1)}, bf16[448,128]{1,0:T(8,128)(2,1)S(1)}, u32[]{:S(2)}, u32[]{:S(2)}) collective-permute-start(bf16[448,128]{1,0:T(8,128)(2,1)S(1)} %bitcast.44), channel_id=1, source_target_pairs={{0,32},{1,33},{2,34},{3,35},{4,36},{5,37},{6,38},{7,39},{8,40},{9,... | collective-permute-start | bytes 344072 | tf_op jit(solution)/shard_map/ppermute | solution.py:355
  77.6 2.6 %collective-permute-done.3 = bf16[1728,128]{1,0:T(8,128)(2,1)S(1)} collective-permute-done((bf16[1728,128]{1,0:T(8,128)(2,1)S(1)}, bf16[1728,128]{1,0:T(8,128)(2,1)S(1)}, u32[]{:S(2)}, u32[]{:S(2)}) %collective-permute-start.3) | collective-permute-done | bytes 442400 | tf_op jit(solution)/shard_map/ppermute | solution.py:353
  80.4 4.4 %collective-permute-start.4 = (bf16[2112,128]{1,0:T(8,128)(2,1)S(1)}, bf16[2112,128]{1,0:T(8,128)(2,1)}, u32[]{:S(2)}, u32[]{:S(2)}) collective-permute-start(bf16[2112,128]{1,0:T(8,128)(2,1)S(1)} %pad_maximum_fusion), channel_id=1, source_target_pairs={{0,32},{32,0},{1,33},{33,1},{2,34},{34,2},{3,35},{35,3},{4,36},{36... | collective-permute-start | bytes 1622024 | tf_op jit(solution)/shard_map/ppermute | solution.py:357
  84.8 1.1 broadcast_in_dim.5
  85.9 6.8 %all-to-all-start.1 = ((bf16[8,8,16,512]{3,2,1,0:T(8,128)(2,1)}), bf16[8,8,16,512]{3,2,1,0:T(8,128)(2,1)S(1)}, u32[]{:S(2)}, u32[]{:S(2)}) async-start(bf16[8,8,16,512]{3,2,1,0:T(8,128)(2,1)} %broadcast_in_dim.5), calls=%async_computation.1 | async-start | bytes 2097152 | tf_op jit(solution)/shard_map/all_to_all | solution.py:340
  92.8 1.4 %collective-permute-start.6 = (bf16[448,128]{1,0:T(8,128)(2,1)S(1)}, bf16[448,128]{1,0:T(8,128)(2,1)S(1)}, u32[]{:S(2)}, u32[]{:S(2)}) collective-permute-start(bf16[448,128]{1,0:T(8,128)(2,1)S(1)} %broadcast_select_fusion.4), channel_id=1, source_target_pairs={{0,16},{1,17},{2,18},{3,19},{4,20},{5,21},{6,22},{7,23},{8,24},{9,... | collective-permute-start | bytes 344072 | tf_op jit(solution)/shard_map/ppermute | solution.py:359
  94.3 1.1 fusion.1
  95.3 5.7 %collective-permute-done.6 = bf16[448,128]{1,0:T(8,128)(2,1)S(1)} collective-permute-done((bf16[448,128]{1,0:T(8,128)(2,1)S(1)}, bf16[448,128]{1,0:T(8,128)(2,1)S(1)}, u32[]{:S(2)}, u32[]{:S(2)}) %collective-permute-start.6) | collective-permute-done | bytes 114720 | tf_op jit(solution)/shard_map/ppermute | solution.py:359
  101.1 1.0 slice_dynamic-update-slice_fusion.near_hbm
  102.1 9.7 %collective-permute-start.7 = (bf16[3328,128]{1,0:T(8,128)(2,1)S(1)}, bf16[3328,128]{1,0:T(8,128)(2,1)}, u32[]{:S(2)}, u32[]{:S(2)}) collective-permute-start(bf16[3328,128]{1,0:T(8,128)(2,1)S(1)} %slice_dynamic-update-slice_fusion.near_hbm), channel_id=1, source_target_pairs={{0,8},{8,0},{1,9},{9,1},{2,10},{10,2},{3,11},{11,3},{4,12},{12,4},... | collective-permute-start | bytes 2555912 | tf_op jit(solution)/shard_map/ppermute | solution.py:361
  112.1 0.7 concatenate.42.info
  112.7 1.2 collective-permute-done.7.other_hbm
  113.9 10.8 %upper_levels.1 = bf16[256,2048]{1,0:T(8,128)(2,1)} custom-call(s32[359]{0:T(512)} %concatenate.42.info, bf16[8,248,256]{2,1,0:T(8,128)(2,1)} %bitcast.35, bf16[8,8,16,512]{3,2,1,0:T(8,128)(2,1)} %copy-done.1, bf16[3328,128]{1,0:T(8,128)(2,1)} %copy-done.2, bf16[3328,128]{1,0:T(8,128)(2,1)} %collective-permute-done.7.other_hbm, bf16[7,256,256]{2,1,0:T(8,128)(2,1)} %pivots.1, ...), custom_call_target="tpu_custom_call" | custom-call | tf_op jit(solution)/shard_map/upper_levels/pallas_call | solution.py:271
  (58 shorter events, 1.2 us)
Async XLA Ops:
  0.0 6.5 %collective-permute-start = (bf16[256,256]{1,0:T(8,128)(2,1)}, bf16[256,256]{1,0:T(8,128)(2,1)S(1)}, u32[]{:S(2)}, u32[]{:S(2)}) collective-permute-start(bf16[256,256]{1,0:T(8,128)(2,1)} %param.6), channel_id=1, source_target_pairs={{0,16},{1,17},{2,18},{3,19},{4,20},{5,21},{6,22},{7,23},{8,24},{9,... | collective-permute-start | bytes 393224 | tf_op jit(solution)/shard_map/ppermute | solution.py:295
  6.5 5.5 %collective-permute-start.1 = (bf16[256,256]{1,0:T(8,128)(2,1)S(1)}, bf16[256,256]{1,0:T(8,128)(2,1)S(1)}, u32[]{:S(2)}, u32[]{:S(2)}) collective-permute-start(bf16[256,256]{1,0:T(8,128)(2,1)S(1)} %broadcast_select_fusion), channel_id=1, source_target_pairs={{0,32},{1,33},{2,34},{3,35},{4,36},{5,37},{6,38},{7,39},{8,40},{9,... | collective-permute-start | bytes 393224 | tf_op jit(solution)/shard_map/ppermute | solution.py:296
  12.0 5.3 %collective-permute-start.2 = (bf16[256,256]{1,0:T(8,128)(2,1)S(1)}, bf16[256,256]{1,0:T(8,128)(2,1)S(1)}, u32[]{:S(2)}, u32[]{:S(2)}) collective-permute-start(bf16[256,256]{1,0:T(8,128)(2,1)S(1)} %broadcast_select_fusion.1), channel_id=1, source_target_pairs={{0,8},{8,0},{1,9},{9,1},{2,10},{10,2},{3,11},{11,3},{4,12},{12,4},... | collective-permute-start | bytes 393224 | tf_op jit(solution)/shard_map/ppermute | solution.py:297
  18.6 14.6 %all-to-all-start = ((bf16[8,32,896]{2,1,0:T(8,128)(2,1)}), bf16[8,32,896]{2,1,0:T(8,128)(2,1)S(1)}, u32[]{:S(2)}, u32[]{:S(2)}) async-start(bf16[8,32,896]{2,1,0:T(8,128)(2,1)} %broadcast_in_dim.4), calls=%async_computation | async-start | bytes 917504 | tf_op jit(solution)/shard_map/all_to_all | solution.py:311
  71.1 13.7 %copy-start = (bf16[1984,256]{1,0:T(8,128)(2,1)}, bf16[1984,256]{1,0:T(8,128)(2,1)S(1)}, u32[]{:S(2)}) copy-start(bf16[1984,256]{1,0:T(8,128)(2,1)S(1)} %all-gather) | copy-start | bytes 3047428
  71.2 9.0 %collective-permute-start.3 = (bf16[1728,128]{1,0:T(8,128)(2,1)S(1)}, bf16[1728,128]{1,0:T(8,128)(2,1)S(1)}, u32[]{:S(2)}, u32[]{:S(2)}) collective-permute-start(bf16[1728,128]{1,0:T(8,128)(2,1)S(1)} %pad_maximum_fusion.1), channel_id=1, source_target_pairs={{0,16},{16,0},{1,17},{17,1},{2,18},{18,2},{3,19},{19,3},{4,20},{20... | collective-permute-start | bytes 1327112 | tf_op jit(solution)/shard_map/ppermute | solution.py:353
  73.6 19.2 %collective-permute-start.5 = (bf16[448,128]{1,0:T(8,128)(2,1)S(1)}, bf16[448,128]{1,0:T(8,128)(2,1)S(1)}, u32[]{:S(2)}, u32[]{:S(2)}) collective-permute-start(bf16[448,128]{1,0:T(8,128)(2,1)S(1)} %bitcast.44), channel_id=1, source_target_pairs={{0,32},{1,33},{2,34},{3,35},{4,36},{5,37},{6,38},{7,39},{8,40},{9,... | collective-permute-start | bytes 344072 | tf_op jit(solution)/shard_map/ppermute | solution.py:355
  80.4 13.8 %collective-permute-start.4 = (bf16[2112,128]{1,0:T(8,128)(2,1)S(1)}, bf16[2112,128]{1,0:T(8,128)(2,1)}, u32[]{:S(2)}, u32[]{:S(2)}) collective-permute-start(bf16[2112,128]{1,0:T(8,128)(2,1)S(1)} %pad_maximum_fusion), channel_id=1, source_target_pairs={{0,32},{32,0},{1,33},{33,1},{2,34},{34,2},{3,35},{35,3},{4,36},{36... | collective-permute-start | bytes 1622024 | tf_op jit(solution)/shard_map/ppermute | solution.py:357
  85.9 26.8 %all-to-all-start.1 = ((bf16[8,8,16,512]{3,2,1,0:T(8,128)(2,1)}), bf16[8,8,16,512]{3,2,1,0:T(8,128)(2,1)S(1)}, u32[]{:S(2)}, u32[]{:S(2)}) async-start(bf16[8,8,16,512]{3,2,1,0:T(8,128)(2,1)} %broadcast_in_dim.5), calls=%async_computation.1 | async-start | bytes 2097152 | tf_op jit(solution)/shard_map/all_to_all | solution.py:340
  92.8 19.0 %copy-start.3 = (s32[4,2,14]{2,1,0:T(2,128)S(1)}, s32[4,2,14]{2,1,0:T(2,128)}, u32[]{:S(2)}) copy-start(s32[4,2,14]{2,1,0:T(2,128)} %param.9) | copy-start | bytes 1348
  92.8 19.1 %copy-start.4 = (s32[2,2,30]{2,1,0:T(2,128)S(1)}, s32[2,2,30]{2,1,0:T(2,128)}, u32[]{:S(2)}) copy-start(s32[2,2,30]{2,1,0:T(2,128)} %param.10) | copy-start | bytes 1444
  92.8 19.2 %copy-start.5 = (s32[1,2,62]{2,1,0:T(2,128)S(1)}, s32[1,2,62]{2,1,0:T(2,128)}, u32[]{:S(2)}) copy-start(s32[1,2,62]{2,1,0:T(2,128)} %param.11) | copy-start | bytes 1492
  92.8 8.2 %collective-permute-start.6 = (bf16[448,128]{1,0:T(8,128)(2,1)S(1)}, bf16[448,128]{1,0:T(8,128)(2,1)S(1)}, u32[]{:S(2)}, u32[]{:S(2)}) collective-permute-start(bf16[448,128]{1,0:T(8,128)(2,1)S(1)} %broadcast_select_fusion.4), channel_id=1, source_target_pairs={{0,16},{1,17},{2,18},{3,19},{4,20},{5,21},{6,22},{7,23},{8,24},{9,... | collective-permute-start | bytes 344072 | tf_op jit(solution)/shard_map/ppermute | solution.py:359
  102.1 11.8 %copy-start.2 = (bf16[3328,128]{1,0:T(8,128)(2,1)}, bf16[3328,128]{1,0:T(8,128)(2,1)S(1)}, u32[]{:S(2)}) copy-start(bf16[3328,128]{1,0:T(8,128)(2,1)S(1)} %slice_dynamic-update-slice_fusion.near_hbm) | copy-start | bytes 2555908
  102.1 11.8 %collective-permute-start.7 = (bf16[3328,128]{1,0:T(8,128)(2,1)S(1)}, bf16[3328,128]{1,0:T(8,128)(2,1)}, u32[]{:S(2)}, u32[]{:S(2)}) collective-permute-start(bf16[3328,128]{1,0:T(8,128)(2,1)S(1)} %slice_dynamic-update-slice_fusion.near_hbm), channel_id=1, source_target_pairs={{0,8},{8,0},{1,9},{9,1},{2,10},{10,2},{3,11},{11,3},{4,12},{12,4},... | collective-permute-start | bytes 2555912 | tf_op jit(solution)/shard_map/ppermute | solution.py:361
  112.7 1.2 copy-start.1

commit v5 on v4

--- a/solution.py
+++ b/solution.py
@@ -10,7 +10,7 @@
 F32 = jnp.float32
 BF16 = jnp.bfloat16
 CORE_AT = 8 * 224
-SPLIT = 6 * 224
+SPLIT = 7 * 224
 MAP_START = (3, 3 + 112, 3 + 112 + 120)
 
 

time: 125 us -> 128 us (1.024)
  waiting for transfers between devices: 24.2 us -> 28.1 us
  starting transfers between devices: 44.7 us -> 42.9 us
    ppermute x1, waiting for transfers between devices: 2.65 us -> 7.33 us  [local(): far = lax.ppermute(jnp.concatenate([first, core], 0), 'xl', swap)]
    ppermute x1, starting transfers between devices: 4.04 us -> 1.92 us  [local(): two = jnp.where(zl == 0, second, lax.ppermute(second, 'zl', down))]
where the time goes in v5:
time: 128 us
  starting transfers between devices  42.9 us (34%)
  blocking collectives  34.9 us (27%)
  waiting for transfers between devices  28.1 us (22%)
  Pallas kernels  10.8 us (8%)
  local copies, waits for them, and re-layouts  6.5 us (5%)
  matrix products  2.66 us (2%)
  other arithmetic  1.44 us (1%)
    all_gather x1, blocking collectives, local(): whole = lax.all_gather(payload, 'k')  34.9 us
    pallas_call x1, Pallas kernels, upper_levels(): pl.pallas_call(upper_kernel, out_shape=jax.ShapeDtypeStruct((256, 2048),...  10.8 us
    ppermute x1, starting transfers between devices, local(): other = lax.ppermute(near, 'c', swap)  9.38 us
    all_to_all x1, waiting for transfers between devices, leaf_stage(): lax.all_to_all(jnp.broadcast_to(piece[None], (8,) + piece.shape), 'sub',...  7.67 us
    all_to_all x1, starting transfers between devices, local(): lax.all_to_all(jnp.broadcast_to(piece[None], (8, 8, 16, 512)), 'sub', 0,...  7.47 us
    ppermute x1, waiting for transfers between devices, local(): far = lax.ppermute(jnp.concatenate([first, core], 0), 'xl', swap)  7.33 us
    all_to_all x1, starting transfers between devices, leaf_stage(): lax.all_to_all(jnp.broadcast_to(piece[None], (8,) + piece.shape), 'sub',...  6.87 us
    ppermute x1, waiting for transfers between devices, leaf_stage(): spread = jnp.where(xl == 0, tile, lax.ppermute(tile, 'xl', [(0, 1)]))  5.16 us
  transfers between devices with their start and end apart: 10, of which 7 were waited for; matrix products, arithmetic and copies ran while one was open for 4% of the time, Pallas kernels for 0%

profile of v5, /device:TPU:7, one launch (start us, length us, event | category | flops | bytes accessed | tf_op | source)
XLA Modules:
  0.0 127.7 jit_solution(16827898815414073559)
XLA Ops:
  0.0 1.3 %collective-permute-start = (bf16[256,256]{1,0:T(8,128)(2,1)}, bf16[256,256]{1,0:T(8,128)(2,1)S(1)}, u32[]{:S(2)}, u32[]{:S(2)}) collective-permute-start(bf16[256,256]{1,0:T(8,128)(2,1)} %param.6), channel_id=1, source_target_pairs={{0,16},{1,17},{2,18},{3,19},{4,20},{5,21},{6,22},{7,23},{8,24},{9,... | collective-permute-start | bytes 393224 | tf_op jit(solution)/shard_map/ppermute | solution.py:295
  1.3 5.2 %collective-permute-done = bf16[256,256]{1,0:T(8,128)(2,1)S(1)} collective-permute-done((bf16[256,256]{1,0:T(8,128)(2,1)}, bf16[256,256]{1,0:T(8,128)(2,1)S(1)}, u32[]{:S(2)}, u32[]{:S(2)}) %collective-permute-start) | collective-permute-done | bytes 131104 | tf_op jit(solution)/shard_map/ppermute | solution.py:295
  6.5 3.5 %collective-permute-start.1 = (bf16[256,256]{1,0:T(8,128)(2,1)S(1)}, bf16[256,256]{1,0:T(8,128)(2,1)S(1)}, u32[]{:S(2)}, u32[]{:S(2)}) collective-permute-start(bf16[256,256]{1,0:T(8,128)(2,1)S(1)} %broadcast_select_fusion), channel_id=1, source_target_pairs={{0,32},{1,33},{2,34},{3,35},{4,36},{5,37},{6,38},{7,39},{8,40},{9,... | collective-permute-start | bytes 393224 | tf_op jit(solution)/shard_map/ppermute | solution.py:296
  10.0 1.0 copy.12
  11.1 0.9 collective-permute-done.1
  12.0 4.3 %collective-permute-start.2 = (bf16[256,256]{1,0:T(8,128)(2,1)S(1)}, bf16[256,256]{1,0:T(8,128)(2,1)S(1)}, u32[]{:S(2)}, u32[]{:S(2)}) collective-permute-start(bf16[256,256]{1,0:T(8,128)(2,1)S(1)} %broadcast_select_fusion.1), channel_id=1, source_target_pairs={{0,8},{8,0},{1,9},{9,1},{2,10},{10,2},{3,11},{11,3},{4,12},{12,4},... | collective-permute-start | bytes 393224 | tf_op jit(solution)/shard_map/ppermute | solution.py:297
  16.3 1.0 collective-permute-done.2
  17.5 0.1 copy.16
  17.8 0.8 broadcast_in_dim.4
  18.6 6.9 %all-to-all-start = ((bf16[8,32,896]{2,1,0:T(8,128)(2,1)}), bf16[8,32,896]{2,1,0:T(8,128)(2,1)S(1)}, u32[]{:S(2)}, u32[]{:S(2)}) async-start(bf16[8,32,896]{2,1,0:T(8,128)(2,1)} %broadcast_in_dim.4), calls=%async_computation | async-start | bytes 917504 | tf_op jit(solution)/shard_map/all_to_all | solution.py:311
  25.6 7.7 %all-to-all-done = bf16[8,32,896]{2,1,0:T(8,128)(2,1)S(1)} async-done(((bf16[8,32,896]{2,1,0:T(8,128)(2,1)}), bf16[8,32,896]{2,1,0:T(8,128)(2,1)S(1)}, u32[]{:S(2)}, u32[]{:S(2)}) %all-to-all-start) | async-done | bytes 458784 | tf_op jit(solution)/shard_map/all_to_all | solution.py:311
  33.3 1.0 convolution_convert_fusion.1
  34.3 0.2 subtract_convert_fusion
  34.6 1.0 convolution_convert_fusion
  35.5 0.2 fusion.8
  35.8 0.2 fusion
  36.1 34.9 %all-gather = bf16[1984,256]{1,0:T(8,128)(2,1)S(1)} all-gather(bf16[248,256]{1,0:T(8,128)(2,1)S(1)} %maximum_maximum_fusion), channel_id=2, replica_groups=mesh['k'=8,'zl'=2,'xl'=2,'c'=2,'sub'=8] {'k'}, dimensions={0}, use_global_device_ids=true | all-gather | bytes 1142784 | tf_op jit(solution)/shard_map/all_gather | solution.py:338
  71.2 2.3 %collective-permute-start.3 = (bf16[1952,128]{1,0:T(8,128)(2,1)S(1)}, bf16[1952,128]{1,0:T(8,128)(2,1)S(1)}, u32[]{:S(2)}, u32[]{:S(2)}) collective-permute-start(bf16[1952,128]{1,0:T(8,128)(2,1)S(1)} %pad_maximum_fusion.1), channel_id=1, source_target_pairs={{0,16},{16,0},{1,17},{17,1},{2,18},{18,2},{3,19},{19,3},{4,20},{20... | collective-permute-start | bytes 1499144 | tf_op jit(solution)/shard_map/ppermute | solution.py:353
  73.6 7.3 %collective-permute-done.3 = bf16[1952,128]{1,0:T(8,128)(2,1)S(1)} collective-permute-done((bf16[1952,128]{1,0:T(8,128)(2,1)S(1)}, bf16[1952,128]{1,0:T(8,128)(2,1)S(1)}, u32[]{:S(2)}, u32[]{:S(2)}) %collective-permute-start.3) | collective-permute-done | bytes 499744 | tf_op jit(solution)/shard_map/ppermute | solution.py:353
  81.1 4.4 %collective-permute-start.4 = (bf16[2336,128]{1,0:T(8,128)(2,1)S(1)}, bf16[2336,128]{1,0:T(8,128)(2,1)}, u32[]{:S(2)}, u32[]{:S(2)}) collective-permute-start(bf16[2336,128]{1,0:T(8,128)(2,1)S(1)} %pad_maximum_fusion), channel_id=1, source_target_pairs={{0,32},{32,0},{1,33},{33,1},{2,34},{34,2},{3,35},{35,3},{4,36},{36... | collective-permute-start | bytes 1794056 | tf_op jit(solution)/shard_map/ppermute | solution.py:357
  85.4 1.9 %collective-permute-start.5 = (bf16[224,128]{1,0:T(8,128)(2,1)S(1)}, bf16[224,128]{1,0:T(8,128)(2,1)S(1)}, u32[]{:S(2)}, u32[]{:S(2)}) collective-permute-start(bf16[224,128]{1,0:T(8,128)(2,1)S(1)} %slice_bitcast_fusion.2), channel_id=1, source_target_pairs={{0,32},{1,33},{2,34},{3,35},{4,36},{5,37},{6,38},{7,39},{8,40},{9,... | collective-permute-start | bytes 172040 | tf_op jit(solution)/shard_map/ppermute | solution.py:355
  87.4 1.1 broadcast_in_dim.5
  88.5 7.5 %all-to-all-start.1 = ((bf16[8,8,16,512]{3,2,1,0:T(8,128)(2,1)}), bf16[8,8,16,512]{3,2,1,0:T(8,128)(2,1)}, u32[]{:S(2)}, u32[]{:S(2)}) async-start(bf16[8,8,16,512]{3,2,1,0:T(8,128)(2,1)} %broadcast_in_dim.5), calls=%async_computation.1 | async-start | bytes 2097152 | tf_op jit(solution)/shard_map/all_to_all | solution.py:340
  96.0 1.4 %collective-permute-start.6 = (bf16[224,128]{1,0:T(8,128)(2,1)S(1)}, bf16[224,128]{1,0:T(8,128)(2,1)S(1)}, u32[]{:S(2)}, u32[]{:S(2)}) collective-permute-start(bf16[224,128]{1,0:T(8,128)(2,1)S(1)} %broadcast_select_fusion.4), channel_id=1, source_target_pairs={{0,16},{1,17},{2,18},{3,19},{4,20},{5,21},{6,22},{7,23},{8,24},{9,... | collective-permute-start | bytes 172040 | tf_op jit(solution)/shard_map/ppermute | solution.py:359
  97.5 1.1 fusion.1
  98.6 5.1 %collective-permute-done.6 = bf16[224,128]{1,0:T(8,128)(2,1)S(1)} collective-permute-done((bf16[224,128]{1,0:T(8,128)(2,1)S(1)}, bf16[224,128]{1,0:T(8,128)(2,1)S(1)}, u32[]{:S(2)}, u32[]{:S(2)}) %collective-permute-start.6) | collective-permute-done | bytes 57376 | tf_op jit(solution)/shard_map/ppermute | solution.py:359
  103.7 1.0 slice_dynamic-update-slice_fusion.near_hbm
  104.7 9.4 %collective-permute-start.7 = (bf16[3328,128]{1,0:T(8,128)(2,1)S(1)}, bf16[3328,128]{1,0:T(8,128)(2,1)S(1)}, u32[]{:S(2)}, u32[]{:S(2)}) collective-permute-start(bf16[3328,128]{1,0:T(8,128)(2,1)S(1)} %slice_dynamic-update-slice_fusion.near_hbm), channel_id=1, source_target_pairs={{0,8},{8,0},{1,9},{9,1},{2,10},{10,2},{3,11},{11,3},{4,12},{12,4},... | collective-permute-start | bytes 2555912 | tf_op jit(solution)/shard_map/ppermute | solution.py:361
  114.3 0.7 concatenate.42.info
  115.0 1.0 collective-permute-done.7.other_hbm
  116.1 0.9 copy-done.2
  117.0 10.8 %upper_levels.1 = bf16[256,2048]{1,0:T(8,128)(2,1)} custom-call(s32[359]{0:T(512)} %concatenate.42.info, bf16[8,248,256]{2,1,0:T(8,128)(2,1)} %bitcast.38, bf16[8,8,16,512]{3,2,1,0:T(8,128)(2,1)} %all-to-all-done.1.got_hbm, bf16[3328,128]{1,0:T(8,128)(2,1)} %copy-done.1, bf16[3328,128]{1,0:T(8,128)(2,1)} %copy-done.2, bf16[7,256,256]{2,1,0:T(8,128)(2,1)} %pivots.1, ...), custom_call_target="tpu_custom_call" | custom-call | tf_op jit(solution)/shard_map/upper_levels/pallas_call | solution.py:271
  (58 shorter events, 1.3 us)
Async XLA Ops:
  0.0 6.5 %collective-permute-start = (bf16[256,256]{1,0:T(8,128)(2,1)}, bf16[256,256]{1,0:T(8,128)(2,1)S(1)}, u32[]{:S(2)}, u32[]{:S(2)}) collective-permute-start(bf16[256,256]{1,0:T(8,128)(2,1)} %param.6), channel_id=1, source_target_pairs={{0,16},{1,17},{2,18},{3,19},{4,20},{5,21},{6,22},{7,23},{8,24},{9,... | collective-permute-start | bytes 393224 | tf_op jit(solution)/shard_map/ppermute | solution.py:295
  6.5 5.5 %collective-permute-start.1 = (bf16[256,256]{1,0:T(8,128)(2,1)S(1)}, bf16[256,256]{1,0:T(8,128)(2,1)S(1)}, u32[]{:S(2)}, u32[]{:S(2)}) collective-permute-start(bf16[256,256]{1,0:T(8,128)(2,1)S(1)} %broadcast_select_fusion), channel_id=1, source_target_pairs={{0,32},{1,33},{2,34},{3,35},{4,36},{5,37},{6,38},{7,39},{8,40},{9,... | collective-permute-start | bytes 393224 | tf_op jit(solution)/shard_map/ppermute | solution.py:296
  12.0 5.3 %collective-permute-start.2 = (bf16[256,256]{1,0:T(8,128)(2,1)S(1)}, bf16[256,256]{1,0:T(8,128)(2,1)S(1)}, u32[]{:S(2)}, u32[]{:S(2)}) collective-permute-start(bf16[256,256]{1,0:T(8,128)(2,1)S(1)} %broadcast_select_fusion.1), channel_id=1, source_target_pairs={{0,8},{8,0},{1,9},{9,1},{2,10},{10,2},{3,11},{11,3},{4,12},{12,4},... | collective-permute-start | bytes 393224 | tf_op jit(solution)/shard_map/ppermute | solution.py:297
  18.6 14.6 %all-to-all-start = ((bf16[8,32,896]{2,1,0:T(8,128)(2,1)}), bf16[8,32,896]{2,1,0:T(8,128)(2,1)S(1)}, u32[]{:S(2)}, u32[]{:S(2)}) async-start(bf16[8,32,896]{2,1,0:T(8,128)(2,1)} %broadcast_in_dim.4), calls=%async_computation | async-start | bytes 917504 | tf_op jit(solution)/shard_map/all_to_all | solution.py:311
  71.1 24.9 %copy-start = (bf16[1984,256]{1,0:T(8,128)(2,1)}, bf16[1984,256]{1,0:T(8,128)(2,1)S(1)}, u32[]{:S(2)}) copy-start(bf16[1984,256]{1,0:T(8,128)(2,1)S(1)} %all-gather) | copy-start | bytes 3047428
  71.2 9.7 %collective-permute-start.3 = (bf16[1952,128]{1,0:T(8,128)(2,1)S(1)}, bf16[1952,128]{1,0:T(8,128)(2,1)S(1)}, u32[]{:S(2)}, u32[]{:S(2)}) collective-permute-start(bf16[1952,128]{1,0:T(8,128)(2,1)S(1)} %pad_maximum_fusion.1), channel_id=1, source_target_pairs={{0,16},{16,0},{1,17},{17,1},{2,18},{18,2},{3,19},{19,3},{4,20},{20... | collective-permute-start | bytes 1499144 | tf_op jit(solution)/shard_map/ppermute | solution.py:353
  81.1 16.4 %collective-permute-start.4 = (bf16[2336,128]{1,0:T(8,128)(2,1)S(1)}, bf16[2336,128]{1,0:T(8,128)(2,1)}, u32[]{:S(2)}, u32[]{:S(2)}) collective-permute-start(bf16[2336,128]{1,0:T(8,128)(2,1)S(1)} %pad_maximum_fusion), channel_id=1, source_target_pairs={{0,32},{32,0},{1,33},{33,1},{2,34},{34,2},{3,35},{35,3},{4,36},{36... | collective-permute-start | bytes 1794056 | tf_op jit(solution)/shard_map/ppermute | solution.py:357
  85.4 10.5 %collective-permute-start.5 = (bf16[224,128]{1,0:T(8,128)(2,1)S(1)}, bf16[224,128]{1,0:T(8,128)(2,1)S(1)}, u32[]{:S(2)}, u32[]{:S(2)}) collective-permute-start(bf16[224,128]{1,0:T(8,128)(2,1)S(1)} %slice_bitcast_fusion.2), channel_id=1, source_target_pairs={{0,32},{1,33},{2,34},{3,35},{4,36},{5,37},{6,38},{7,39},{8,40},{9,... | collective-permute-start | bytes 172040 | tf_op jit(solution)/shard_map/ppermute | solution.py:355
  88.5 26.5 %all-to-all-start.1 = ((bf16[8,8,16,512]{3,2,1,0:T(8,128)(2,1)}), bf16[8,8,16,512]{3,2,1,0:T(8,128)(2,1)}, u32[]{:S(2)}, u32[]{:S(2)}) async-start(bf16[8,8,16,512]{3,2,1,0:T(8,128)(2,1)} %broadcast_in_dim.5), calls=%async_computation.1 | async-start | bytes 2097152 | tf_op jit(solution)/shard_map/all_to_all | solution.py:340
  96.0 18.1 %copy-start.3 = (s32[4,2,14]{2,1,0:T(2,128)S(1)}, s32[4,2,14]{2,1,0:T(2,128)}, u32[]{:S(2)}) copy-start(s32[4,2,14]{2,1,0:T(2,128)} %param.9) | copy-start | bytes 1348
  96.0 18.2 %copy-start.4 = (s32[2,2,30]{2,1,0:T(2,128)S(1)}, s32[2,2,30]{2,1,0:T(2,128)}, u32[]{:S(2)}) copy-start(s32[2,2,30]{2,1,0:T(2,128)} %param.10) | copy-start | bytes 1444
  96.0 18.2 %copy-start.5 = (s32[1,2,62]{2,1,0:T(2,128)S(1)}, s32[1,2,62]{2,1,0:T(2,128)}, u32[]{:S(2)}) copy-start(s32[1,2,62]{2,1,0:T(2,128)} %param.11) | copy-start | bytes 1492
  96.0 7.6 %collective-permute-start.6 = (bf16[224,128]{1,0:T(8,128)(2,1)S(1)}, bf16[224,128]{1,0:T(8,128)(2,1)S(1)}, u32[]{:S(2)}, u32[]{:S(2)}) collective-permute-start(bf16[224,128]{1,0:T(8,128)(2,1)S(1)} %broadcast_select_fusion.4), channel_id=1, source_target_pairs={{0,16},{1,17},{2,18},{3,19},{4,20},{5,21},{6,22},{7,23},{8,24},{9,... | collective-permute-start | bytes 172040 | tf_op jit(solution)/shard_map/ppermute | solution.py:359
  104.7 11.4 %copy-start.1 = (bf16[3328,128]{1,0:T(8,128)(2,1)}, bf16[3328,128]{1,0:T(8,128)(2,1)S(1)}, u32[]{:S(2)}) copy-start(bf16[3328,128]{1,0:T(8,128)(2,1)S(1)} %slice_dynamic-update-slice_fusion.near_hbm) | copy-start | bytes 2555908
  104.7 11.4 %collective-permute-start.7 = (bf16[3328,128]{1,0:T(8,128)(2,1)S(1)}, bf16[3328,128]{1,0:T(8,128)(2,1)S(1)}, u32[]{:S(2)}, u32[]{:S(2)}) collective-permute-start(bf16[3328,128]{1,0:T(8,128)(2,1)S(1)} %slice_dynamic-update-slice_fusion.near_hbm), channel_id=1, source_target_pairs={{0,8},{8,0},{1,9},{9,1},{2,10},{10,2},{3,11},{11,3},{4,12},{12,4},... | collective-permute-start | bytes 2555912 | tf_op jit(solution)/shard_map/ppermute | solution.py:361
  116.1 0.9 copy-start.2
